TPU v7x, 256 devices: a whole 4x4x8 slice. The times are simulated.
256 devices in a mesh: grp: 2 (over core), tp: 16 (over x, y), tok: 8 (over z).
Axes of the slice: x: 4, y: 4, z: 8, core: 2. Of those that a mesh axis runs over, the one named last changes fastest.
Arguments:
- teacher_hidden: bfloat16 [256, 16384], P('tok', 'tp'), may hold values from -6 to 6
- teacher_gain: float32 [16384], replicated, may hold values from 0.25 to 1.75
- teacher_head: bfloat16 [16384, 65536], P(None, ('grp', 'tp', 'tok')), may hold values from -1 to 1
- student_hidden: bfloat16 [256, 4096], P('tok', 'tp'), may hold values from -6 to 6
- student_gain: float32 [4096], replicated, may hold values from 0.25 to 1.75
- student_head: bfloat16 [4096, 65536], P(None, ('grp', 'tp', 'tok')), may hold values from -1 to 1
- targets: int32 [256], replicated, may hold values from 0 to 65535
Outputs:
- loss: float32 [256], replicated
- d_student_head: bfloat16 [4096, 65536], P(None, ('grp', 'tp', 'tok'))
- d_student_hidden: bfloat16 [256, 4096], P(('tp', 'tok'))
- d_student_gain: float32 [4096], replicated
All inputs are finite; a program needn't handle non-finite values.
Results may differ from a plain program's by a relative error of at most 0.0067.
Values may be sent and summed in bfloat16 or wider, within the bound.
No kernel may reach another device: no remote copies, remote signals or barrier semaphores. Data moves between devices by JAX's collectives and lax.ppermute only.
A program may use at most 64 MiB of HBM per device.

v0:
```python
import jax
import jax.numpy as jnp
from jax import lax
from jax.sharding import PartitionSpec as P

EPS = 1e-05
ALPHA = 0.0625
LOSS_SCALE = 4096.0


def rms_norm(hidden, gain):
    input_values = hidden.astype(jnp.float32)
    inverse_rms_scale = lax.rsqrt(
        jnp.mean(input_values * input_values, axis=1, keepdims=True) + EPS
    )
    return (input_values * inverse_rms_scale * gain).astype(jnp.bfloat16)


def norm_backward(hidden_rows, normed_gradient, gain):
    input_values = hidden_rows.astype(jnp.float32)
    row_scale_factors = lax.rsqrt(
        jnp.mean(input_values * input_values, axis=1, keepdims=True) + EPS
    )
    normalized_input = input_values * row_scale_factors
    incoming_gradient = normed_gradient * gain
    hidden_gradient = (
        row_scale_factors
        * (
            incoming_gradient
            - normalized_input
            * jnp.mean(incoming_gradient * normalized_input, axis=1, keepdims=True)
        )
    ).astype(jnp.bfloat16)
    return (hidden_gradient, jnp.sum(normed_gradient * normalized_input, axis=0))


def on_device(
    teacher_hidden, teacher_gain, teacher_head, student_hidden, student_gain, student_head, targets
):
    wide = lax.all_gather(teacher_hidden, "tp", axis=1, tiled=True)
    teacher_logits = jnp.dot(
        rms_norm(lax.all_gather(wide, "tok", axis=0, tiled=True), teacher_gain),
        teacher_head,
        preferred_element_type=jnp.float32,
    )
    student_cols = lax.all_gather(student_hidden, "tp", axis=1, tiled=True)
    student_full = lax.all_gather(student_cols, "tok", axis=0, tiled=True)
    student_normed = rms_norm(student_full, student_gain)
    student_logits = jnp.dot(student_normed, student_head, preferred_element_type=jnp.float32)
    top_t, top_s = lax.pmax(
        (jnp.max(teacher_logits, axis=1), jnp.max(student_logits, axis=1)), ("grp", "tp", "tok")
    )
    sums_t = jnp.sum(jnp.exp(teacher_logits - top_t[:, None]), axis=1)
    sums_s = jnp.sum(jnp.exp(student_logits - top_s[:, None]), axis=1)
    total_t, total_s = lax.psum((sums_t, sums_s), ("grp", "tp", "tok"))
    lse_t = top_t + jnp.log(total_t)
    lse_s = top_s + jnp.log(total_s)
    log_t = teacher_logits - lse_t[:, None]
    log_s = student_logits - lse_s[:, None]
    p_t = jnp.exp(log_t)
    p_s = jnp.exp(log_s)
    voc_width = student_head.shape[1]
    columns = lax.axis_index(("grp", "tp", "tok")) * voc_width + jnp.arange(
        voc_width, dtype=jnp.int32
    )
    onehot = columns[None, :] == targets[:, None]
    kl_part = jnp.sum(p_t * (log_t - log_s), axis=1)
    target_part = jnp.sum(jnp.where(onehot, student_logits, jnp.float32(0.0)), axis=1)
    kl_sum, target_logit = lax.psum((kl_part, target_part), ("grp", "tp", "tok"))
    loss = kl_sum + ALPHA * (lse_s - target_logit)
    grad_logits = (
        LOSS_SCALE * ((1.0 + ALPHA) * p_s - p_t - ALPHA * onehot.astype(jnp.float32))
    ).astype(jnp.bfloat16)
    d_head = lax.dot_general(
        student_normed, grad_logits, (((0,), (0,)), ((), ())), preferred_element_type=jnp.float32
    ).astype(jnp.bfloat16)
    block_rows = student_full.shape[0] // lax.axis_size(("tp", "tok"))
    partial_rows = lax.psum_scatter(
        lax.dot_general(
            grad_logits, student_head, (((1,), (1,)), ((), ())), preferred_element_type=jnp.float32
        ),
        ("tp", "tok"),
        scatter_dimension=0,
        tiled=True,
    )
    normed_gradient = lax.psum(partial_rows, "grp")
    own_rows = lax.dynamic_slice_in_dim(
        student_full, lax.axis_index(("tp", "tok")) * block_rows, block_rows, 0
    )
    hidden_gradient, gain_part = norm_backward(own_rows, normed_gradient, student_gain)
    gain_gradient = lax.psum(gain_part, ("tp", "tok"))
    return (loss, d_head, hidden_gradient, gain_gradient)


def solution(mesh):
    placed = (
        P("tok", "tp"),
        P(),
        P(None, ("grp", "tp", "tok")),
        P("tok", "tp"),
        P(),
        P(None, ("grp", "tp", "tok")),
        P(),
    )
    return jax.shard_map(
        on_device,
        mesh=mesh,
        in_specs=placed,
        out_specs=(P(), P(None, ("grp", "tp", "tok")), P(("tp", "tok"), None), P()),
        check_vma=False,
    )
```

profile of v0, /device:TPU:0, one launch (start us, length us, event | category | flops | bytes accessed | tf_op | source)
XLA Modules:
  0.0 1294.5 jit_solution(3926361760504066683)
XLA Ops:
  7.2 0.7 all-gather.4.cloned.1.call-update
  8.0 24.9 %all_gather.14 = bf16[32,4096]{1,0:T(8,128)(2,1)} all-gather(bf16[32,256]{1,0:T(8,128)(2,1)} %param.10), channel_id=1, replica_groups=mesh['grp'=2,'tp'=16,'tok'=8] {'tp'}, dimensions={1}, use_global_device_ids=true | all-gather | bytes 278528 | tf_op jit(solution)/shard_map/all_gather | solution.py:46
  32.9 26.5 %all-gather.4.cloned.1.call-done = bf16[32,16384]{1,0:T(8,128)(2,1)} async-done(((bf16[32,1024]{1,0:T(8,128)(2,1)}), bf16[32,16384]{1,0:T(8,128)(2,1)}) %all-gather.4.cloned.1.call-update) | async-done | bytes 1048592 | tf_op jit(solution)/shard_map/all_gather | solution.py:40
  59.6 42.1 %all-gather.8.cloned.1.call-done = bf16[256,4096]{1,0:T(8,128)(2,1)} async-done(((bf16[32,4096]{1,0:T(8,128)(2,1)}), bf16[256,4096]{1,0:T(8,128)(2,1)}) %all-gather.8.cloned.1.call-update) | async-done | bytes 2097168 | tf_op jit(solution)/shard_map/all_gather | solution.py:47
  101.7 2.1 fusion.7
  103.8 2.7 fusion.26
  106.6 89.7 %all-gather.6.cloned.1.call-done = bf16[256,16384]{1,0:T(8,128)(2,1)} async-done(((bf16[32,16384]{1,0:T(8,128)(2,1)}), bf16[256,16384]{1,0:T(8,128)(2,1)}) %all-gather.6.cloned.1.call-update) | async-done | bytes 8388624 | tf_op jit(solution)/shard_map/all_gather | solution.py:42
  196.2 5.1 fusion
  201.4 9.8 fusion.27
  211.2 76.6 %all-reduce.3 = (f32[256]{0:T(256)S(1)}, f32[256]{0:T(256)S(1)}) all-reduce(f32[256]{0:T(256)S(1)} %get-tuple-element.15, f32[256]{0:T(256)S(1)} %get-tuple-element.17), channel_id=1, replica_groups=mesh['grp'=2,'tp'=16,'tok'=8] {'grp','tp','tok'}, use_global_device_ids=true, to_apply=%region_7.0 | all-reduce | flops 512 | bytes 4096 | tf_op jit(solution)/shard_map/pmax | solution.py:50
  287.8 72.1 %all-reduce.2 = (f32[256]{0:T(256)S(1)}, f32[256]{0:T(256)S(1)}) all-reduce(f32[256]{0:T(256)S(1)} %get-tuple-element.19, f32[256]{0:T(256)S(1)} %get-tuple-element.20), channel_id=1, replica_groups=mesh['grp'=2,'tp'=16,'tok'=8] {'grp','tp','tok'}, use_global_device_ids=true, to_apply=%region_9.0 | all-reduce | flops 512 | bytes 4096 | tf_op jit(solution)/shard_map/psum | solution.py:55
  360.0 0.2 fusion.13
  360.2 2.7 fusion.28
  363.0 0.6 dynamic-slice
  364.2 1.0 fusion.24
  365.2 75.1 %all-reduce.1 = (f32[256]{0:T(256)S(1)}, f32[256]{0:T(256)S(1)}) all-reduce(f32[256]{0:T(256)S(1)} %get-tuple-element.7, f32[256]{0:T(256)S(1)} %get-tuple-element.6), channel_id=1, replica_groups=mesh['grp'=2,'tp'=16,'tok'=8] {'grp','tp','tok'}, use_global_device_ids=true, to_apply=%region_11.12 | all-reduce | flops 512 | bytes 4096 | tf_op jit(solution)/shard_map/psum | solution.py:69
  440.3 0.6 multiply_add_fusion
  440.9 3.9 convolution_convert_fusion
  444.7 150.4 %all-reduce.6.cloned.1.call-done = f32[256,4096]{1,0:T(8,128)} async-done(((f32[256,4096]{1,0:T(8,128)}), f32[256,4096]{1,0:T(8,128)}) %all-reduce.6.cloned.1.call-update) | async-done | bytes 4194320
  595.1 0.9 constant_dynamic-slice_fusion
  596.1 3.4 psum.46
  599.5 1.1 fusion.23
  600.6 685.9 %psum.47 = f32[4096]{0:T(1024)} all-reduce(f32[4096]{0:T(1024)S(1)} %get-tuple-element.4), channel_id=1, replica_groups=mesh['grp'=2,'tp'=16,'tok'=8] {'tp','tok'}, use_global_device_ids=true, to_apply=%region_19.20 | all-reduce | flops 4096 | bytes 32768 | tf_op jit(solution)/shard_map/psum | solution.py:91
  1286.5 1.5 fusion.25
  (25 shorter events, 0.4 us)
Async XLA Ops:
  7.2 96.7 %copy-start = (bf16[4096,256]{1,0:T(8,128)(2,1)S(1)}, bf16[4096,256]{1,0:T(8,128)(2,1)}, u32[]{:S(2)}) copy-start(bf16[4096,256]{1,0:T(8,128)(2,1)} %param.12) | copy-start | bytes 6291460
  7.2 52.3 %all-gather.4.cloned.1.call-start = ((), (), s32[]{:S(2)}) async-start(), calls=%async_computation | async-start | bytes 1114112 | tf_op jit(solution)/shard_map/all_gather | solution.py:40
  7.9 93.8 %all-gather.8.cloned.1.call-start = ((), (), s32[]{:S(2)}) async-start(), calls=%async_computation.2 | async-start | bytes 2359296 | tf_op jit(solution)/shard_map/all_gather | solution.py:47
  32.9 163.3 %all-gather.6.cloned.1.call-start = ((), (), s32[]{:S(2)}) async-start(), calls=%async_computation.1 | async-start | bytes 9437184 | tf_op jit(solution)/shard_map/all_gather | solution.py:42
  59.5 535.6 %all-reduce.6.cloned.1.call-start = ((), (), s32[]{:S(2)}) async-start(), calls=%async_computation.3 | async-start | bytes 8388608
  106.5 94.8 %copy-start.3 = (f32[16384]{0:T(1024)S(1)}, f32[16384]{0:T(1024)}, u32[]{:S(2)}) copy-start(f32[16384]{0:T(1024)} %param.8) | copy-start | bytes 196612
  201.4 158.6 %copy-start.2 = (s32[256]{0:T(256)S(1)}, s32[256]{0:T(256)}, u32[]{:S(2)}) copy-start(s32[256]{0:T(256)} %param.13) | copy-start | bytes 3076
  360.1 2.8 copy-start.4
  360.1 80.7 %copy-start.1 = (f32[4096]{0:T(1024)S(1)}, f32[4096]{0:T(1024)}, u32[]{:S(2)}) copy-start(f32[4096]{0:T(1024)} %param.11) | copy-start | bytes 49156
Sparse Core Ops, SparseCore 0:
  10.5 48.9 all-gather.3
  61.3 40.4 all-gather.7
  103.5 92.6 all-gather.5
  363.1 232.0 all-reduce.5
where the time goes:
time: 1300 us; the launch traced here: 1290 us
  blocking collectives  938 us (72%)
  waiting for transfers between devices  310 us (24%)
  matrix products  19.1 us (1%)
  between operations  14.5 us (1%)
    psum x1, blocking collectives, on_device(): gain_gradient = lax.psum(gain_part, ('tp', 'tok'))  686 us
    unnamed x5, waiting for transfers between devices  151 us
    all_gather x1, waiting for transfers between devices, on_device(): lax.all_gather(wide, 'tok', axis=0, tiled=True)  89.7 us
    pmax x1, blocking collectives, on_device(): lax.pmax((jnp.max(teacher_logits, axis=1), jnp.max(student_logits, axis=1...  76.6 us
    psum x1, blocking collectives, on_device(): lax.psum((kl_part, target_part), ('grp', 'tp', 'tok'))  75.1 us
    psum x1, blocking collectives, on_device(): total_t, total_s = lax.psum((sums_t, sums_s), ('grp', 'tp', 'tok'))  72.1 us
    all_gather x1, waiting for transfers between devices, on_device(): student_full = lax.all_gather(student_cols, 'tok', axis=0, tiled=True)  42.1 us
    all_gather x1, waiting for transfers between devices, on_device(): wide = lax.all_gather(teacher_hidden, 'tp', axis=1, tiled=True)  26.5 us
  transfers between devices with their start and end apart: 4, of which 4 were waited for; matrix products, arithmetic and copies ran while one was open for 1% of the time, Pallas kernels for 0%

commit v1 on v0

v1 whole, which is shorter than its diff:
```python
import functools

import jax
import jax.numpy as jnp
from jax import lax
from jax.experimental import pallas as pl
from jax.experimental.pallas import tpu as pltpu
from jax.sharding import PartitionSpec as P

EPS = 1e-05
ALPHA = 0.0625
LOSS_SCALE = 4096.0
AXES = ("grp", "tp", "tok")
F32 = jnp.float32
BF16 = jnp.bfloat16
VMEM_LIMIT = 48 * 1024 * 1024
NX, NY, NZ = 4, 4, 8
NTP = NX * NY
TOKENS = 256
KT = 512
KS = 128
VOC = 256


def permute(value, move):
    pairs = []
    for g in range(2):
        for x in range(NX):
            for y in range(NY):
                for z in range(NZ):
                    g2, x2, y2, z2 = move(g, x, y, z)
                    source = (g * NTP + x * NY + y) * NZ + z
                    target = ((g2 % 2) * NTP + (x2 % NX) * NY + y2 % NY) * NZ + z2 % NZ
                    pairs.append((source, target))
    return lax.ppermute(value, AXES, pairs)


def swap_cores(value):
    return permute(value, lambda g, x, y, z: (g + 1, x, y, z))


def shift_z(value, d):
    return permute(value, lambda g, x, y, z: (g, x, y, z + d))


def shift_first(value, d):
    return permute(value, lambda g, x, y, z: (g, x, y + d, z) if g == 0 else (g, x + d, y, z))


def shift_second(value, d):
    return permute(value, lambda g, x, y, z: (g, x + d, y, z) if g == 0 else (g, x, y + d, z))


def params(limit=VMEM_LIMIT):
    return pltpu.CompilerParams(vmem_limit_bytes=limit)


def dot(a, b, dims):
    return lax.dot_general(a, b, (dims, ((), ())), preferred_element_type=F32)


def logits_kernel(
    where, own, back, fore, far_a, far_b, r_t, r_s, gain_t, gain_s, w_own, w_oth, s_own, s_oth,
    logits, normed_s, raw_s,
):
    j = pl.program_id(0)
    g = where[16]

    @pl.when(j == 0)
    def _():
        logits[...] = jnp.zeros_like(logits)

    def step(block):
        h_t = block[0, :, :KT].astype(F32)
        n_t = (h_t * r_t[...] * gain_t[0]).astype(BF16)
        h_s = block[0, :, KT:]
        n_s = (h_s.astype(F32) * r_s[...] * gain_s[0]).astype(BF16)
        normed_s[0] = n_s
        raw_s[0] = h_s
        mine = pl.ds(pl.multiple_of(g * VOC, VOC), VOC)
        other = pl.ds(pl.multiple_of((1 - g) * VOC, VOC), VOC)
        nn = ((1,), (0,))
        logits[0, :, mine] += dot(n_t, w_own[0, 0], nn)
        logits[0, :, other] += dot(n_t, w_oth[0], nn)
        logits[1, :, mine] += dot(n_s, s_own[0, 0], nn)
        logits[1, :, other] += dot(n_s, s_oth[0], nn)

    for ref, low, high in (
        (own, 0, 4), (back, 4, 8), (fore, 8, 12), (far_a, 12, 14), (far_b, 14, 16),
    ):
        pl.when((j >= low) & (j < high))(functools.partial(step, ref))


def partial_logits(where, pieces, r_t, r_s, gain_t, gain_s, w4, w_oth, s4, s_oth):
    def piece(low, count):
        return pl.BlockSpec(
            (1, TOKENS, KT + KS), lambda j, w: (jnp.clip(j - low, 0, count - 1), 0, 0)
        )

    column = pl.BlockSpec((TOKENS, 1), lambda j, w: (0, 0))
    grid_spec = pltpu.PrefetchScalarGridSpec(
        num_scalar_prefetch=1,
        grid=(16,),
        in_specs=[
            piece(0, 4), piece(4, 4), piece(8, 4), piece(12, 2), piece(14, 2), column, column,
            pl.BlockSpec((1, 1, KT), lambda j, w: (w[j] * 2 + w[16], 0, 0)),
            pl.BlockSpec((1, 1, KS), lambda j, w: (w[j] * 2 + w[16], 0, 0)),
            pl.BlockSpec((1, 1, KT, VOC), lambda j, w: (w[j], w[16], 0, 0)),
            pl.BlockSpec((1, KT, VOC), lambda j, w: (w[j], 0, 0)),
            pl.BlockSpec((1, 1, KS, VOC), lambda j, w: (w[j], w[16], 0, 0)),
            pl.BlockSpec((1, KS, VOC), lambda j, w: (w[j], 0, 0)),
        ],
        out_specs=[
            pl.BlockSpec((2, TOKENS, 2 * VOC), lambda j, w: (0, 0, 0)),
            pl.BlockSpec((1, TOKENS, KS), lambda j, w: (w[j], 0, 0)),
            pl.BlockSpec((1, TOKENS, KS), lambda j, w: (w[j], 0, 0)),
        ],
    )
    return pl.pallas_call(
        logits_kernel,
        grid_spec=grid_spec,
        out_shape=[
            jax.ShapeDtypeStruct((2, TOKENS, 2 * VOC), F32),
            jax.ShapeDtypeStruct((NTP, TOKENS, KS), BF16),
            jax.ShapeDtypeStruct((NTP, TOKENS, KS), BF16),
        ],
        compiler_params=params(),
    )(where, *pieces, r_t, r_s, gain_t, gain_s, w4, w_oth, s4, s_oth)


def onehot_of(targets, base):
    lane = lax.broadcasted_iota(jnp.int32, (TOKENS, 2 * VOC), 1)
    column = jnp.where(lane < VOC, base[0] + lane, base[1] + lane - VOC)
    return column == targets


def stats_kernel(base, mine, other, targets, both, records):
    t = mine[0] + other[0]
    s = mine[1] + other[1]
    both[0] = t
    both[1] = s

    def row_sum(v):
        return jnp.sum(v, axis=1, keepdims=True)

    m_t = jnp.max(t, axis=1, keepdims=True)
    m_s = jnp.max(s, axis=1, keepdims=True)
    e_t = jnp.exp(t - m_t)
    hit = onehot_of(targets[...], base)
    columns = [
        m_t, row_sum(e_t), row_sum(e_t * (t - s)), m_s, row_sum(jnp.exp(s - m_s)),
        row_sum(jnp.where(hit, s, 0.0)),
    ]
    lane = lax.broadcasted_iota(jnp.int32, (TOKENS, 128), 1)
    packed = jnp.zeros((TOKENS, 128), F32)
    for k, column in enumerate(columns):
        packed = jnp.where(lane == k, column, packed)
    rows = jnp.transpose(packed)[:8]
    for k in range(NTP):
        records[k] = rows


def local_stats(base, mine, other, targets):
    vmem = pl.BlockSpec(memory_space=pltpu.VMEM)
    return pl.pallas_call(
        stats_kernel,
        in_specs=[pl.BlockSpec(memory_space=pltpu.SMEM), vmem, vmem, vmem],
        out_specs=[vmem, vmem],
        out_shape=[
            jax.ShapeDtypeStruct((2, TOKENS, 2 * VOC), F32),
            jax.ShapeDtypeStruct((NTP, 8, TOKENS), F32),
        ],
        compiler_params=params(),
    )(base, mine, other, targets)


def merged(records):
    m_t, z_t, a, m_s, z_s, hit = (records[:, k, :] for k in range(6))
    top_t = jnp.max(m_t, axis=0, keepdims=True)
    top_s = jnp.max(m_s, axis=0, keepdims=True)
    w_t = jnp.exp(m_t - top_t)
    w_s = jnp.exp(m_s - top_s)

    def total(v):
        return jnp.sum(v, axis=0, keepdims=True)

    return top_t, total(w_t * z_t), total(w_t * a), top_s, total(w_s * z_s), total(hit)


def merge_kernel(copies, records, out):
    rows = merged(records[...])
    for c in range(copies):
        for k in range(6):
            out[c, k : k + 1, :] = rows[k]
        out[c, 6:8, :] = jnp.zeros((2, TOKENS), F32)


def merge_records(records, copies):
    vmem = pl.BlockSpec(memory_space=pltpu.VMEM)
    return pl.pallas_call(
        functools.partial(merge_kernel, copies),
        in_specs=[vmem],
        out_specs=vmem,
        out_shape=jax.ShapeDtypeStruct((copies, 8, TOKENS), F32),
        compiler_params=params(),
    )(records)


def grad_kernel(
    base, records, both, targets, r_s, raw_s, s_own, s_oth, parts, gain_hi, gain_lo, grad_own, loss, grads
):
    j = pl.program_id(0)
    g = base[2]

    @pl.when(j == 0)
    def _():
        top_t, z_t, a, top_s, z_s, hit = merged(records[...])
        lse_t = top_t + jnp.log(z_t)
        lse_s = top_s + jnp.log(z_s)
        loss[...] = a / z_t - lse_t + lse_s + ALPHA * (lse_s - hit)
        row = lax.broadcasted_iota(jnp.int32, (128, TOKENS), 0)
        packed = jnp.where(row == 0, lse_t, jnp.where(row == 1, lse_s, 0.0))
        columns = jnp.transpose(packed)
        p_t = jnp.exp(both[0] - columns[:, 0:1])
        p_s = jnp.exp(both[1] - columns[:, 1:2])
        hits = onehot_of(targets[...], base).astype(F32)
        grad = (LOSS_SCALE * ((1.0 + ALPHA) * p_s - p_t - ALPHA * hits)).astype(BF16)
        grads[0] = grad[:, :VOC]
        grads[1] = grad[:, VOC:]
        grad_own[...] = grads[g]

    nt = ((1,), (1,))
    for k in range(4):
        part = dot(grads[g], s_own[k, 0], nt) + dot(grads[1 - g], s_oth[k], nt)
        parts[:, k * 16 : (k + 1) * 16, :] = part.astype(BF16).reshape(NTP, 16, KS)
        xhat = raw_s[k].astype(F32) * r_s[...]
        gain = jnp.sum(part * xhat, axis=0, keepdims=True)
        high = gain.astype(BF16)
        gain_hi[k] = high
        gain_lo[k] = (gain - high.astype(F32)).astype(BF16)


def grad_parts(base, records, both, targets, r_s, raw_s, s4, s_oth):
    whole = lambda *shape: pl.BlockSpec(shape, lambda j, b: (0,) * len(shape))
    grid_spec = pltpu.PrefetchScalarGridSpec(
        num_scalar_prefetch=1,
        grid=(4,),
        in_specs=[
            whole(NZ, 8, TOKENS), whole(2, TOKENS, 2 * VOC), whole(TOKENS, 1), whole(TOKENS, 1),
            pl.BlockSpec((4, TOKENS, KS), lambda j, b: (j, 0, 0)),
            pl.BlockSpec((4, 1, KS, VOC), lambda j, b: (j, b[2], 0, 0)),
            pl.BlockSpec((4, KS, VOC), lambda j, b: (j, 0, 0)),
        ],
        out_specs=[
            pl.BlockSpec((NTP, 64, KS), lambda j, b: (0, j, 0)),
            pl.BlockSpec((4, 1, KS), lambda j, b: (j, 0, 0)),
            pl.BlockSpec((4, 1, KS), lambda j, b: (j, 0, 0)),
            whole(TOKENS, VOC), whole(1, TOKENS),
        ],
        scratch_shapes=[pltpu.VMEM((2, TOKENS, VOC), BF16)],
    )
    return pl.pallas_call(
        grad_kernel,
        grid_spec=grid_spec,
        out_shape=[
            jax.ShapeDtypeStruct((NTP, 256, KS), BF16),
            jax.ShapeDtypeStruct((NTP, 1, KS), BF16),
            jax.ShapeDtypeStruct((NTP, 1, KS), BF16),
            jax.ShapeDtypeStruct((TOKENS, VOC), BF16),
            jax.ShapeDtypeStruct((1, TOKENS), F32),
        ],
        compiler_params=params(),
    )(base, records, both, targets, r_s, raw_s, s4, s_oth)


def head_kernel(base, mine, other, grad, out):
    g = base[2]
    tn = ((0,), (0,))
    for k in range(4):
        out[k, g] = dot(mine[k], grad[...], tn).astype(BF16)
        out[k, 1 - g] = dot(other[k], grad[...], tn).astype(BF16)


def head_gradient(base, mine, other, grad):
    block = pl.BlockSpec((4, TOKENS, KS), lambda j, b: (j, 0, 0))
    grid_spec = pltpu.PrefetchScalarGridSpec(
        num_scalar_prefetch=1,
        grid=(4,),
        in_specs=[block, block, pl.BlockSpec((TOKENS, VOC), lambda j, b: (0, 0))],
        out_specs=pl.BlockSpec((4, 2, KS, VOC), lambda j, b: (j, 0, 0, 0)),
    )
    return pl.pallas_call(
        head_kernel,
        grid_spec=grid_spec,
        out_shape=jax.ShapeDtypeStruct((NTP, 2, KS, VOC), BF16),
        compiler_params=params(),
    )(base, mine, other, grad)


def fold_kernel(parts, out, total):
    acc = parts[0].astype(F32)
    for k in range(1, NTP):
        acc = acc + parts[k].astype(F32)
    total[...] = acc
    gain = total[256:272, :] + total[272:288, :]
    for z in range(NZ):
        for i in range(2):
            out[z, i * 16 : (i + 1) * 16, :] = total[pl.ds(2 * z + i, 16, stride=16), :]
        out[z, 32:48, :] = gain


def fold_parts(parts):
    vmem = pl.BlockSpec(memory_space=pltpu.VMEM)
    return pl.pallas_call(
        fold_kernel,
        in_specs=[vmem],
        out_specs=vmem,
        out_shape=jax.ShapeDtypeStruct((NZ, 48, KS), F32),
        scratch_shapes=[pltpu.VMEM((288, KS), F32)],
        compiler_params=params(),
    )(parts)


def sum_kernel(parts, rows, out):
    acc = parts[0]
    for k in range(1, NZ):
        acc = acc + parts[k]
    out[0:48, :] = acc
    out[48:80, :] = rows[...]


def sum_parts(parts, rows):
    vmem = pl.BlockSpec(memory_space=pltpu.VMEM)
    return pl.pallas_call(
        sum_kernel,
        in_specs=[vmem, vmem],
        out_specs=vmem,
        out_shape=jax.ShapeDtypeStruct((80, KS), F32),
        compiler_params=params(),
    )(parts, rows)


def norm_backward(halves, gain):
    def tokens(v):
        return v.reshape(2, 2, NTP, KS).transpose(1, 2, 0, 3).reshape(2, 2 * NTP * KS)

    normed_gradient = tokens(halves[:, 0:32])
    input_values = tokens(halves[:, 48:80])
    gain_gradient = halves[:, 32:48].transpose(1, 0, 2).reshape(2 * NTP * KS)
    scale = lax.rsqrt(jnp.mean(input_values * input_values, axis=1, keepdims=True) + EPS)
    xhat = input_values * scale
    dy = normed_gradient * gain
    hidden_gradient = scale * (dy - xhat * jnp.mean(dy * xhat, axis=1, keepdims=True))
    return hidden_gradient.astype(BF16), gain_gradient


def on_device(
    teacher_hidden, teacher_gain, teacher_head, student_hidden, student_gain, student_head, targets
):
    g = lax.axis_index("grp")
    tp = lax.axis_index("tp")
    z = lax.axis_index("tok")
    x, y = tp // NY, tp % NY

    w4 = teacher_head.reshape(NTP, 2, KT, VOC)
    s4 = student_head.reshape(NTP, 2, KS, VOC)
    w_oth = swap_cores(lax.dynamic_index_in_dim(w4, 1 - g, 1, keepdims=False))
    s_oth = swap_cores(lax.dynamic_index_in_dim(s4, 1 - g, 1, keepdims=False))

    rows = teacher_hidden.shape[0]
    block = jnp.concatenate(
        [
            lax.dynamic_slice_in_dim(teacher_hidden, g * KT, KT, 1),
            lax.dynamic_slice_in_dim(student_hidden, g * KS, KS, 1),
        ],
        axis=1,
    )
    by_shift = [block] + [shift_z(block, d) for d in range(1, NZ)]
    ahead = [by_shift[(-i) % NZ] for i in range(NZ)]
    slab = lax.dynamic_slice_in_dim(
        jnp.concatenate(ahead + ahead, axis=0), ((NZ - z) % NZ) * rows, TOKENS, 0
    )
    own = jnp.stack([slab] + [shift_first(slab, d) for d in (1, 2, 3)])
    back = shift_second(own, 1)
    fore = shift_second(own, -1)
    far_a = shift_second(back[:2], 1)
    far_b = shift_second(fore[2:], -1)
    pieces = (own, back, fore, far_a, far_b)

    def squares(low, high):
        total = 0.0
        for piece in pieces:
            v = piece[:, :, low:high].astype(F32)
            total = total + jnp.sum(v * v, axis=(0, 2))
        return total

    squares_half = jnp.stack([squares(0, KT), squares(KT, KT + KS)])
    squares_all = squares_half + swap_cores(squares_half)
    width = jnp.array([teacher_gain.shape[0], student_gain.shape[0]], F32)[:, None]
    scales = lax.rsqrt(squares_all / width + EPS)
    r_t, r_s = scales[0][:, None], scales[1][:, None]

    a_pos = jnp.where(g == 0, x, y)
    b_pos = jnp.where(g == 0, y, x)
    a_abs = (a_pos + jnp.array([0, -1, 1, 2], jnp.int32)[:, None]) % 4
    b_abs = (b_pos - jnp.arange(4, dtype=jnp.int32)[None, :]) % 4
    place = jnp.where(g == 0, a_abs * NY + b_abs, b_abs * NY + a_abs).reshape(16)
    where = jnp.concatenate([place, g[None]]).astype(jnp.int32)
    half, normed_s, raw_s = partial_logits(
        where, pieces, r_t, r_s, teacher_gain.reshape(32, 1, KT), student_gain.reshape(32, 1, KS),
        w4, w_oth, s4, s_oth,
    )
    normed_oth = swap_cores(normed_s)
    chip = (tp * NZ + z) * VOC
    base = jnp.stack([chip, NTP * NZ * VOC + chip, g]).astype(jnp.int32)
    targets_column = targets[:, None]
    both, records = local_stats(base, half, swap_cores(half), targets_column)
    records = lax.all_to_all(records, "tp", 0, 0, tiled=True)
    records = lax.all_to_all(merge_records(records, NZ), "tok", 0, 0, tiled=True)
    parts, gain_hi, gain_lo, grad_own, loss = grad_parts(
        base, records, both, targets_column, r_s, raw_s, s4, s_oth
    )
    d_head = head_gradient(base, normed_s, normed_oth, grad_own)

    gain_rows = jnp.concatenate([gain_hi[:, 0], gain_lo[:, 0]], axis=0)
    outgoing = jnp.concatenate(
        [parts, jnp.broadcast_to(gain_rows[None], (NTP, 32, KS))], axis=1
    )
    arrived = lax.all_to_all(outgoing, "tp", 0, 0, tiled=True)
    arrived = lax.all_to_all(fold_parts(arrived), "tok", 0, 0, tiled=True)
    hidden_rows = lax.dynamic_slice_in_dim(raw_s, tp * 16 + z * 2, 2, 1)
    hidden_rows = hidden_rows.astype(F32).transpose(1, 0, 2).reshape(32, KS)
    mine = sum_parts(arrived, hidden_rows)
    other = swap_cores(mine)
    halves = jnp.where(g == 0, jnp.stack([mine, other]), jnp.stack([other, mine]))
    hidden_gradient, gain_gradient = norm_backward(halves, student_gain)
    return (
        loss.reshape(TOKENS),
        d_head.reshape(student_head.shape),
        hidden_gradient,
        gain_gradient,
    )


def solution(mesh):
    placed = (
        P("tok", "tp"),
        P(),
        P(None, ("grp", "tp", "tok")),
        P("tok", "tp"),
        P(),
        P(None, ("grp", "tp", "tok")),
        P(),
    )
    return jax.shard_map(
        on_device,
        mesh=mesh,
        in_specs=placed,
        out_specs=(P(), P(None, ("grp", "tp", "tok")), P(("tp", "tok"), None), P()),
        check_vma=False,
    )
```

time: 1300 us -> 173 us (0.13)
  the two profiles are of different devices: /device:TPU:0 before, /device:TPU:1 now
where the time goes in v1:
time: 173 us; the launch traced here: 172 us
  starting transfers between devices  57.3 us (33%)
  waiting for transfers between devices  43.2 us (25%)
  Pallas kernels  28.5 us (16%)
  blocking collectives  21.1 us (12%)
  local copies, waits for them, and re-layouts  12.2 us (7%)
  other arithmetic  8.91 us (5%)
    ppermute x20, starting transfers between devices, permute(): return lax.ppermute(value, AXES, pairs)  50.1 us
    ppermute x20, waiting for transfers between devices, permute(): return lax.ppermute(value, AXES, pairs)  21.8 us
    pallas_call x1, Pallas kernels, partial_logits(): pl.pallas_call(logits_kernel, grid_spec=grid_spec, out_shape=[jax.ShapeDt...  15.7 us
    all_to_all x1, waiting for transfers between devices, on_device(): arrived = lax.all_to_all(outgoing, 'tp', 0, 0, tiled=True)  12.9 us
    all_to_all x1, blocking collectives, on_device(): lax.all_to_all(merge_records(records, NZ), 'tok', 0, 0, tiled=True)  11.8 us
    all_to_all x1, blocking collectives, on_device(): records = lax.all_to_all(records, 'tp', 0, 0, tiled=True)  9.31 us
    all_to_all x1, waiting for transfers between devices, on_device(): arrived = lax.all_to_all(fold_parts(arrived), 'tok', 0, 0, tiled=True)  8.5 us
    reduce_sum x10, other arithmetic, squares(): total = total + jnp.sum(v * v, axis=(0, 2))  6.23 us
  transfers between devices with their start and end apart: 22, of which 11 were waited for; matrix products, arithmetic and copies ran while one was open for 9% of the time, Pallas kernels for 3%

profile of v1, /device:TPU:1, one launch (start us, length us, event | category | flops | bytes accessed | tf_op | source)
XLA Modules:
  0.0 172.3 jit_solution(13887708730266335929)
XLA Ops:
  1.5 6.5 %collective-permute-start = (bf16[32,640]{1,0:T(8,128)(2,1)S(1)}, bf16[32,640]{1,0:T(8,128)(2,1)S(1)}, u32[]{:S(2)}, u32[]{:S(2)}) collective-permute-start(bf16[32,640]{1,0:T(8,128)(2,1)S(1)} %get-tuple-element.28), channel_id=1, source_target_pairs={{0,7},{1,0},{2,1},{3,2},{4,3},{5,4},{6,5},{7,6},{8,15},{9,8},{10,9... | collective-permute-start | bytes 122888 | tf_op jit(solution)/shard_map/ppermute | solution.py:35
  9.6 4.5 %collective-permute-start.3 = (bf16[32,640]{1,0:T(8,128)(2,1)S(1)}, bf16[32,640]{1,0:T(8,128)(2,1)S(1)}, u32[]{:S(2)}, u32[]{:S(2)}) collective-permute-start(bf16[32,640]{1,0:T(8,128)(2,1)S(1)} %get-tuple-element.28), channel_id=1, source_target_pairs={{0,4},{1,5},{2,6},{3,7},{4,0},{5,1},{6,2},{7,3},{8,12},{9,13},{10,... | collective-permute-start | bytes 122888 | tf_op jit(solution)/shard_map/ppermute | solution.py:35
  17.8 2.2 %collective-permute-done.4 = bf16[32,640]{1,0:T(8,128)(2,1)S(1)} collective-permute-done((bf16[32,640]{1,0:T(8,128)(2,1)S(1)}, bf16[32,640]{1,0:T(8,128)(2,1)S(1)}, u32[]{:S(2)}, u32[]{:S(2)}) %collective-permute-start.4) | collective-permute-done | bytes 40992 | tf_op jit(solution)/shard_map/ppermute | solution.py:35
  21.4 2.6 %collective-permute-start.9 = (bf16[256,640]{1,0:T(8,128)(2,1)S(1)}, bf16[256,640]{1,0:T(8,128)(2,1)S(1)}, u32[]{:S(2)}, u32[]{:S(2)}) collective-permute-start(bf16[256,640]{1,0:T(8,128)(2,1)S(1)} %constant_dynamic-slice_fusion), channel_id=1, source_target_pairs={{0,24},{1,25},{2,26},{3,27},{4,28},{5,29},{6,30},{7,31},{8,0},{9,1... | collective-permute-start | bytes 983048 | tf_op jit(solution)/shard_map/ppermute | solution.py:35
  25.1 4.5 %dynamic-slice_bitcast_fusion = bf16[16,512,256]{2,1,0:T(8,128)(2,1)} fusion(bf16[16,2,512,256]{3,2,1,0:T(8,128)(2,1)} %bitcast.51, s32[]{:T(128)S(6)} %select_n.93), kind=kLoop, calls=%fused_computation | loop fusion | bytes 8388612 | tf_op jit(solution)/shard_map/jit(dynamic_index_in_dim)/squeeze | solution.py:367
  29.6 4.3 %collective-permute-start.15 = (bf16[16,512,256]{2,1,0:T(8,128)(2,1)}, bf16[16,512,256]{2,1,0:T(8,128)(2,1)}, u32[]{:S(2)}, u32[]{:S(2)}) collective-permute-start(bf16[16,512,256]{2,1,0:T(8,128)(2,1)} %dynamic-slice_bitcast_fusion), channel_id=1, source_target_pairs={{0,128},{1,129},{2,130},{3,131},{4,132},{5,133},{6,134},{7,135},{8... | collective-permute-start | bytes 12582920 | tf_op jit(solution)/shard_map/ppermute | solution.py:35
  35.4 2.8 %collective-permute-start.11 = (bf16[4,256,640]{2,1,0:T(8,128)(2,1)S(1)}, bf16[4,256,640]{2,1,0:T(8,128)(2,1)}, u32[]{:S(2)}, u32[]{:S(2)}) collective-permute-start(bf16[4,256,640]{2,1,0:T(8,128)(2,1)S(1)} %pad_maximum_fusion.own), channel_id=1, source_target_pairs={{0,96},{1,97},{2,98},{3,99},{4,100},{5,101},{6,102},{7,103},{8,104... | collective-permute-start | bytes 3932168 | tf_op jit(solution)/shard_map/ppermute | solution.py:35
  39.3 4.7 %collective-permute-start.16 = (bf16[16,128,256]{2,1,0:T(8,128)(2,1)}, bf16[16,128,256]{2,1,0:T(8,128)(2,1)S(1)}, u32[]{:S(2)}, u32[]{:S(2)}) collective-permute-start(bf16[16,128,256]{2,1,0:T(8,128)(2,1)} %dynamic-slice_bitcast_fusion.1), channel_id=1, source_target_pairs={{0,128},{1,129},{2,130},{3,131},{4,132},{5,133},{6,134},{7,135},{8... | collective-permute-start | bytes 3145736 | tf_op jit(solution)/shard_map/ppermute | solution.py:35
  44.5 8.3 %collective-permute-done.11.fore = bf16[4,256,640]{2,1,0:T(8,128)(2,1)} collective-permute-done((bf16[4,256,640]{2,1,0:T(8,128)(2,1)S(1)}, bf16[4,256,640]{2,1,0:T(8,128)(2,1)}, u32[]{:S(2)}, u32[]{:S(2)}) %collective-permute-start.11) | collective-permute-done | bytes 1310752 | tf_op jit(solution)/shard_map/ppermute | solution.py:35
  53.9 3.6 %collective-permute-start.13 = (bf16[2,256,640]{2,1,0:T(8,128)(2,1)S(1)}, bf16[2,256,640]{2,1,0:T(8,128)(2,1)S(1)}, u32[]{:S(2)}, u32[]{:S(2)}) collective-permute-start(bf16[2,256,640]{2,1,0:T(8,128)(2,1)S(1)} %slice.69), channel_id=1, source_target_pairs={{0,96},{1,97},{2,98},{3,99},{4,100},{5,101},{6,102},{7,103},{8,104... | collective-permute-start | bytes 1966088 | tf_op jit(solution)/shard_map/ppermute | solution.py:35
  65.2 4.8 %collective-permute-done.12.far_a = bf16[2,256,640]{2,1,0:T(8,128)(2,1)S(1)} collective-permute-done((bf16[2,256,640]{2,1,0:T(8,128)(2,1)S(1)}, bf16[2,256,640]{2,1,0:T(8,128)(2,1)S(1)}, u32[]{:S(2)}, u32[]{:S(2)}) %collective-permute-start.12) | collective-permute-done | bytes 655392 | tf_op jit(solution)/shard_map/ppermute | solution.py:35
  70.5 6.5 %collective-permute-start.14 = (f32[2,256]{1,0:T(2,128)S(1)}, f32[2,256]{1,0:T(2,128)S(1)}, u32[]{:S(2)}, u32[]{:S(2)}) collective-permute-start(f32[2,256]{1,0:T(2,128)S(1)} %pad_maximum_fusion.4), channel_id=1, source_target_pairs={{0,128},{1,129},{2,130},{3,131},{4,132},{5,133},{6,134},{7,135},{8... | collective-permute-start | bytes 6152 | tf_op jit(solution)/shard_map/ppermute | solution.py:35
  78.3 15.7 %shard_map.120 = (f32[2,256,512]{2,1,0:T(8,128)}, bf16[16,256,128]{2,1,0:T(8,128)(2,1)S(1)}, bf16[16,256,128]{2,1,0:T(8,128)(2,1)S(1)}) custom-call(s32[17]{0:T(128)S(1)} %pad_add_fusion.1.where, bf16[4,256,640]{2,1,0:T(8,128)(2,1)} %copy-done.8, bf16[4,256,640]{2,1,0:T(8,128)(2,1)} %collective-permute-done.10.back, ...), custom_call_target="tpu_custom_call" | custom-call | tf_op jit(solution)/shard_map/pallas_call | solution.py:119
  96.5 2.4 %collective-permute-done.17.other = f32[2,256,512]{2,1,0:T(8,128)} collective-permute-done((f32[2,256,512]{2,1,0:T(8,128)}, f32[2,256,512]{2,1,0:T(8,128)}, u32[]{:S(2)}, u32[]{:S(2)}) %collective-permute-start.17) | collective-permute-done | bytes 1048608 | tf_op jit(solution)/shard_map/ppermute | solution.py:35
  101.0 9.3 %all_to_all.20.records = f32[16,8,256]{2,1,0:T(8,128)S(1)} all-to-all(f32[16,8,256]{2,1,0:T(8,128)S(1)} %get-tuple-element.15), channel_id=1, replica_groups=mesh['grp'=2,'tp'=16,'tok'=8] {'tp'}, dimensions={0} | all-to-all | bytes 262144 | tf_op jit(solution)/shard_map/all_to_all | solution.py:418
  110.4 11.8 %all_to_all.21.records = f32[8,8,256]{2,1,0:T(8,128)S(1)} all-to-all(f32[8,8,256]{2,1,0:T(8,128)S(1)} %shard_map.122), channel_id=1, replica_groups=mesh['grp'=2,'tp'=16,'tok'=8] {'tok'}, dimensions={0} | all-to-all | bytes 131072 | tf_op jit(solution)/shard_map/all_to_all | solution.py:419
  122.2 5.0 %shard_map.123 = (bf16[16,256,128]{2,1,0:T(8,128)(2,1)S(1)}, bf16[16,1,128]{2,1,0:T(2,128)(2,1)S(1)}, bf16[16,1,128]{2,1,0:T(2,128)(2,1)S(1)}, bf16[256,256]{1,0:T(8,128)(2,1)S(1)}, f32[1,256]{1,0:T(1,128)}) custom-call(s32[3]{0:T(128)S(1)} %pad_add_fusion.base, f32[8,8,256]{2,1,0:T(8,128)S(1)} %all_to_all.21.records, ...), custom_call_target="tpu_custom_call" | custom-call | tf_op jit(solution)/shard_map/pallas_call | solution.py:262
  128.3 3.8 %all-to-all-start.2 = ((bf16[16,288,128]{2,1,0:T(8,128)(2,1)}), bf16[16,288,128]{2,1,0:T(8,128)(2,1)S(1)}, u32[]{:S(2)}, u32[]{:S(2)}) async-start(bf16[16,288,128]{2,1,0:T(8,128)(2,1)} %pad_maximum_fusion.1), calls=%async_computation.2 | async-start | bytes 2359296 | tf_op jit(solution)/shard_map/all_to_all | solution.py:429
  132.2 2.9 %collective-permute-start.18 = (bf16[16,256,128]{2,1,0:T(8,128)(2,1)S(1)}, bf16[16,256,128]{2,1,0:T(8,128)(2,1)}, u32[]{:S(2)}, u32[]{:S(2)}) collective-permute-start(bf16[16,256,128]{2,1,0:T(8,128)(2,1)S(1)} %copy-done.4), channel_id=1, source_target_pairs={{0,128},{1,129},{2,130},{3,131},{4,132},{5,133},{6,134},{7,135},{8... | collective-permute-start | bytes 3145736 | tf_op jit(solution)/shard_map/ppermute | solution.py:35
  135.1 12.9 %all-to-all-done.2.parts = bf16[16,288,128]{2,1,0:T(8,128)(2,1)S(1)} async-done(((bf16[16,288,128]{2,1,0:T(8,128)(2,1)}), bf16[16,288,128]{2,1,0:T(8,128)(2,1)S(1)}, u32[]{:S(2)}, u32[]{:S(2)}) %all-to-all-start.2) | async-done | bytes 1179680 | tf_op jit(solution)/shard_map/all_to_all | solution.py:429
  148.8 3.4 %all-to-all-start.3 = ((f32[8,48,128]{2,1,0:T(8,128)}), f32[8,48,128]{2,1,0:T(8,128)S(1)}, u32[]{:S(2)}, u32[]{:S(2)}) async-start(f32[8,48,128]{2,1,0:T(8,128)} %shard_map.125), calls=%async_computation.3 | async-start | bytes 393216 | tf_op jit(solution)/shard_map/all_to_all | solution.py:430
  152.3 8.5 %all-to-all-done.3.parts = f32[8,48,128]{2,1,0:T(8,128)S(1)} async-done(((f32[8,48,128]{2,1,0:T(8,128)}), f32[8,48,128]{2,1,0:T(8,128)S(1)}, u32[]{:S(2)}, u32[]{:S(2)}) %all-to-all-start.3) | async-done | bytes 196640 | tf_op jit(solution)/shard_map/all_to_all | solution.py:430
  160.8 4.9 %collective-permute-start.19 = (f32[80,128]{1,0:T(8,128)S(1)}, f32[80,128]{1,0:T(8,128)S(1)}, u32[]{:S(2)}, u32[]{:S(2)}) collective-permute-start(f32[80,128]{1,0:T(8,128)S(1)} %shard_map.126), channel_id=1, source_target_pairs={{0,128},{1,129},{2,130},{3,131},{4,132},{5,133},{6,134},{7,135},{8... | collective-permute-start | bytes 122888 | tf_op jit(solution)/shard_map/ppermute | solution.py:35
  165.7 4.7 %shard_map.124 = bf16[16,2,128,256]{3,2,1,0:T(8,128)(2,1)} custom-call(s32[3]{0:T(128)S(1)} %pad_add_fusion.base, bf16[16,256,128]{2,1,0:T(8,128)(2,1)S(1)} %copy-done.4, bf16[16,256,128]{2,1,0:T(8,128)(2,1)} %collective-permute-done.18.other, bf16[256,256]{1,0:T(8,128)(2,1)S(1)} %get-tuple-element.20.grad), custom_call_target="tpu_custom_call" | custom-call | tf_op jit(solution)/shard_map/pallas_call | solution.py:292
  (123 shorter events, 30.6 us)
Async XLA Ops:
  1.5 12.6 %collective-permute-start = (bf16[32,640]{1,0:T(8,128)(2,1)S(1)}, bf16[32,640]{1,0:T(8,128)(2,1)S(1)}, u32[]{:S(2)}, u32[]{:S(2)}) collective-permute-start(bf16[32,640]{1,0:T(8,128)(2,1)S(1)} %get-tuple-element.28), channel_id=1, source_target_pairs={{0,7},{1,0},{2,1},{3,2},{4,3},{5,4},{6,5},{7,6},{8,15},{9,8},{10,9... | collective-permute-start | bytes 122888 | tf_op jit(solution)/shard_map/ppermute | solution.py:35
  8.0 8.3 %collective-permute-start.1 = (bf16[32,640]{1,0:T(8,128)(2,1)S(1)}, bf16[32,640]{1,0:T(8,128)(2,1)S(1)}, u32[]{:S(2)}, u32[]{:S(2)}) collective-permute-start(bf16[32,640]{1,0:T(8,128)(2,1)S(1)} %get-tuple-element.28), channel_id=1, source_target_pairs={{0,6},{1,7},{2,0},{3,1},{4,2},{5,3},{6,4},{7,5},{8,14},{9,15},{10,... | collective-permute-start | bytes 122888 | tf_op jit(solution)/shard_map/ppermute | solution.py:35
  9.1 8.6 %collective-permute-start.2 = (bf16[32,640]{1,0:T(8,128)(2,1)S(1)}, bf16[32,640]{1,0:T(8,128)(2,1)S(1)}, u32[]{:S(2)}, u32[]{:S(2)}) collective-permute-start(bf16[32,640]{1,0:T(8,128)(2,1)S(1)} %get-tuple-element.28), channel_id=1, source_target_pairs={{0,5},{1,6},{2,7},{3,0},{4,1},{5,2},{6,3},{7,4},{8,13},{9,14},{10,... | collective-permute-start | bytes 122888 | tf_op jit(solution)/shard_map/ppermute | solution.py:35
  9.6 8.1 %collective-permute-start.3 = (bf16[32,640]{1,0:T(8,128)(2,1)S(1)}, bf16[32,640]{1,0:T(8,128)(2,1)S(1)}, u32[]{:S(2)}, u32[]{:S(2)}) collective-permute-start(bf16[32,640]{1,0:T(8,128)(2,1)S(1)} %get-tuple-element.28), channel_id=1, source_target_pairs={{0,4},{1,5},{2,6},{3,7},{4,0},{5,1},{6,2},{7,3},{8,12},{9,13},{10,... | collective-permute-start | bytes 122888 | tf_op jit(solution)/shard_map/ppermute | solution.py:35
  14.1 5.9 %collective-permute-start.4 = (bf16[32,640]{1,0:T(8,128)(2,1)S(1)}, bf16[32,640]{1,0:T(8,128)(2,1)S(1)}, u32[]{:S(2)}, u32[]{:S(2)}) collective-permute-start(bf16[32,640]{1,0:T(8,128)(2,1)S(1)} %get-tuple-element.28), channel_id=1, source_target_pairs={{0,3},{1,4},{2,5},{3,6},{4,7},{5,0},{6,1},{7,2},{8,11},{9,12},{10,... | collective-permute-start | bytes 122888 | tf_op jit(solution)/shard_map/ppermute | solution.py:35
  14.1 6.9 %collective-permute-start.5 = (bf16[32,640]{1,0:T(8,128)(2,1)S(1)}, bf16[32,640]{1,0:T(8,128)(2,1)S(1)}, u32[]{:S(2)}, u32[]{:S(2)}) collective-permute-start(bf16[32,640]{1,0:T(8,128)(2,1)S(1)} %get-tuple-element.28), channel_id=1, source_target_pairs={{0,2},{1,3},{2,4},{3,5},{4,6},{5,7},{6,0},{7,1},{8,10},{9,11},{10,... | collective-permute-start | bytes 122888 | tf_op jit(solution)/shard_map/ppermute | solution.py:35
  16.3 4.9 %collective-permute-start.6 = (bf16[32,640]{1,0:T(8,128)(2,1)S(1)}, bf16[32,640]{1,0:T(8,128)(2,1)S(1)}, u32[]{:S(2)}, u32[]{:S(2)}) collective-permute-start(bf16[32,640]{1,0:T(8,128)(2,1)S(1)} %get-tuple-element.28), channel_id=1, source_target_pairs={{0,1},{1,2},{2,3},{3,4},{4,5},{5,6},{6,7},{7,0},{8,9},{9,10},{10,1... | collective-permute-start | bytes 122888 | tf_op jit(solution)/shard_map/ppermute | solution.py:35
  21.4 12.5 %collective-permute-start.9 = (bf16[256,640]{1,0:T(8,128)(2,1)S(1)}, bf16[256,640]{1,0:T(8,128)(2,1)S(1)}, u32[]{:S(2)}, u32[]{:S(2)}) collective-permute-start(bf16[256,640]{1,0:T(8,128)(2,1)S(1)} %constant_dynamic-slice_fusion), channel_id=1, source_target_pairs={{0,24},{1,25},{2,26},{3,27},{4,28},{5,29},{6,30},{7,31},{8,0},{9,1... | collective-permute-start | bytes 983048 | tf_op jit(solution)/shard_map/ppermute | solution.py:35
  24.0 10.0 %collective-permute-start.8 = (bf16[256,640]{1,0:T(8,128)(2,1)S(1)}, bf16[256,640]{1,0:T(8,128)(2,1)S(1)}, u32[]{:S(2)}, u32[]{:S(2)}) collective-permute-start(bf16[256,640]{1,0:T(8,128)(2,1)S(1)} %constant_dynamic-slice_fusion), channel_id=1, source_target_pairs={{0,16},{1,17},{2,18},{3,19},{4,20},{5,21},{6,22},{7,23},{8,24},{9,... | collective-permute-start | bytes 983048 | tf_op jit(solution)/shard_map/ppermute | solution.py:35
  24.5 10.7 %collective-permute-start.7 = (bf16[256,640]{1,0:T(8,128)(2,1)S(1)}, bf16[256,640]{1,0:T(8,128)(2,1)S(1)}, u32[]{:S(2)}, u32[]{:S(2)}) collective-permute-start(bf16[256,640]{1,0:T(8,128)(2,1)S(1)} %constant_dynamic-slice_fusion), channel_id=1, source_target_pairs={{0,8},{1,9},{2,10},{3,11},{4,12},{5,13},{6,14},{7,15},{8,16},{9,17... | collective-permute-start | bytes 983048 | tf_op jit(solution)/shard_map/ppermute | solution.py:35
  29.6 48.6 %collective-permute-start.15 = (bf16[16,512,256]{2,1,0:T(8,128)(2,1)}, bf16[16,512,256]{2,1,0:T(8,128)(2,1)}, u32[]{:S(2)}, u32[]{:S(2)}) collective-permute-start(bf16[16,512,256]{2,1,0:T(8,128)(2,1)} %dynamic-slice_bitcast_fusion), channel_id=1, source_target_pairs={{0,128},{1,129},{2,130},{3,131},{4,132},{5,133},{6,134},{7,135},{8... | collective-permute-start | bytes 12582920 | tf_op jit(solution)/shard_map/ppermute | solution.py:35
  35.4 22.1 %copy-start.8 = (bf16[4,256,640]{2,1,0:T(8,128)(2,1)}, bf16[4,256,640]{2,1,0:T(8,128)(2,1)S(1)}, u32[]{:S(2)}) copy-start(bf16[4,256,640]{2,1,0:T(8,128)(2,1)S(1)} %pad_maximum_fusion.own) | copy-start | bytes 3932164
  35.4 17.4 %collective-permute-start.11 = (bf16[4,256,640]{2,1,0:T(8,128)(2,1)S(1)}, bf16[4,256,640]{2,1,0:T(8,128)(2,1)}, u32[]{:S(2)}, u32[]{:S(2)}) collective-permute-start(bf16[4,256,640]{2,1,0:T(8,128)(2,1)S(1)} %pad_maximum_fusion.own), channel_id=1, source_target_pairs={{0,96},{1,97},{2,98},{3,99},{4,100},{5,101},{6,102},{7,103},{8,104... | collective-permute-start | bytes 3932168 | tf_op jit(solution)/shard_map/ppermute | solution.py:35
  38.2 19.4 %collective-permute-start.10 = (bf16[4,256,640]{2,1,0:T(8,128)(2,1)S(1)}, bf16[4,256,640]{2,1,0:T(8,128)(2,1)}, u32[]{:S(2)}, u32[]{:S(2)}) collective-permute-start(bf16[4,256,640]{2,1,0:T(8,128)(2,1)S(1)} %pad_maximum_fusion.own), channel_id=1, source_target_pairs={{0,32},{1,33},{2,34},{3,35},{4,36},{5,37},{6,38},{7,39},{8,40},{9,... | collective-permute-start | bytes 3932168 | tf_op jit(solution)/shard_map/ppermute | solution.py:35
  39.3 38.9 %collective-permute-start.16 = (bf16[16,128,256]{2,1,0:T(8,128)(2,1)}, bf16[16,128,256]{2,1,0:T(8,128)(2,1)S(1)}, u32[]{:S(2)}, u32[]{:S(2)}) collective-permute-start(bf16[16,128,256]{2,1,0:T(8,128)(2,1)} %dynamic-slice_bitcast_fusion.1), channel_id=1, source_target_pairs={{0,128},{1,129},{2,130},{3,131},{4,132},{5,133},{6,134},{7,135},{8... | collective-permute-start | bytes 3145736 | tf_op jit(solution)/shard_map/ppermute | solution.py:35
  53.9 11.1 %collective-permute-start.13 = (bf16[2,256,640]{2,1,0:T(8,128)(2,1)S(1)}, bf16[2,256,640]{2,1,0:T(8,128)(2,1)S(1)}, u32[]{:S(2)}, u32[]{:S(2)}) collective-permute-start(bf16[2,256,640]{2,1,0:T(8,128)(2,1)S(1)} %slice.69), channel_id=1, source_target_pairs={{0,96},{1,97},{2,98},{3,99},{4,100},{5,101},{6,102},{7,103},{8,104... | collective-permute-start | bytes 1966088 | tf_op jit(solution)/shard_map/ppermute | solution.py:35
  58.8 11.2 %collective-permute-start.12 = (bf16[2,256,640]{2,1,0:T(8,128)(2,1)S(1)}, bf16[2,256,640]{2,1,0:T(8,128)(2,1)S(1)}, u32[]{:S(2)}, u32[]{:S(2)}) collective-permute-start(bf16[2,256,640]{2,1,0:T(8,128)(2,1)S(1)} %slice.68), channel_id=1, source_target_pairs={{0,32},{1,33},{2,34},{3,35},{4,36},{5,37},{6,38},{7,39},{8,40},{9,... | collective-permute-start | bytes 1966088 | tf_op jit(solution)/shard_map/ppermute | solution.py:35
  70.5 7.3 %collective-permute-start.14 = (f32[2,256]{1,0:T(2,128)S(1)}, f32[2,256]{1,0:T(2,128)S(1)}, u32[]{:S(2)}, u32[]{:S(2)}) collective-permute-start(f32[2,256]{1,0:T(2,128)S(1)} %pad_maximum_fusion.4), channel_id=1, source_target_pairs={{0,128},{1,129},{2,130},{3,131},{4,132},{5,133},{6,134},{7,135},{8... | collective-permute-start | bytes 6152 | tf_op jit(solution)/shard_map/ppermute | solution.py:35
  95.9 3.0 %collective-permute-start.17 = (f32[2,256,512]{2,1,0:T(8,128)}, f32[2,256,512]{2,1,0:T(8,128)}, u32[]{:S(2)}, u32[]{:S(2)}) collective-permute-start(f32[2,256,512]{2,1,0:T(8,128)} %get-tuple-element.14.mine), channel_id=1, source_target_pairs={{0,128},{1,129},{2,130},{3,131},{4,132},{5,133},{6,134},{7,135},{8... | collective-permute-start | bytes 3145736 | tf_op jit(solution)/shard_map/ppermute | solution.py:35
  96.5 25.7 %copy-start.2 = (bf16[16,256,128]{2,1,0:T(8,128)(2,1)S(1)}, bf16[16,256,128]{2,1,0:T(8,128)(2,1)}, u32[]{:S(2)}) copy-start(bf16[16,256,128]{2,1,0:T(8,128)(2,1)} %copy-done.1) | copy-start | bytes 3145732
  128.3 19.6 %all-to-all-start.2 = ((bf16[16,288,128]{2,1,0:T(8,128)(2,1)}), bf16[16,288,128]{2,1,0:T(8,128)(2,1)S(1)}, u32[]{:S(2)}, u32[]{:S(2)}) async-start(bf16[16,288,128]{2,1,0:T(8,128)(2,1)} %pad_maximum_fusion.1), calls=%async_computation.2 | async-start | bytes 2359296 | tf_op jit(solution)/shard_map/all_to_all | solution.py:429
  132.2 33.6 %collective-permute-start.18 = (bf16[16,256,128]{2,1,0:T(8,128)(2,1)S(1)}, bf16[16,256,128]{2,1,0:T(8,128)(2,1)}, u32[]{:S(2)}, u32[]{:S(2)}) collective-permute-start(bf16[16,256,128]{2,1,0:T(8,128)(2,1)S(1)} %copy-done.4), channel_id=1, source_target_pairs={{0,128},{1,129},{2,130},{3,131},{4,132},{5,133},{6,134},{7,135},{8... | collective-permute-start | bytes 3145736 | tf_op jit(solution)/shard_map/ppermute | solution.py:35
  148.8 11.9 %all-to-all-start.3 = ((f32[8,48,128]{2,1,0:T(8,128)}), f32[8,48,128]{2,1,0:T(8,128)S(1)}, u32[]{:S(2)}, u32[]{:S(2)}) async-start(f32[8,48,128]{2,1,0:T(8,128)} %shard_map.125), calls=%async_computation.3 | async-start | bytes 393216 | tf_op jit(solution)/shard_map/all_to_all | solution.py:430
  160.8 9.7 %collective-permute-start.19 = (f32[80,128]{1,0:T(8,128)S(1)}, f32[80,128]{1,0:T(8,128)S(1)}, u32[]{:S(2)}, u32[]{:S(2)}) collective-permute-start(f32[80,128]{1,0:T(8,128)S(1)} %shard_map.126), channel_id=1, source_target_pairs={{0,128},{1,129},{2,130},{3,131},{4,132},{5,133},{6,134},{7,135},{8... | collective-permute-start | bytes 122888 | tf_op jit(solution)/shard_map/ppermute | solution.py:35
  (10 other events, 82.2 us)

commit v2 on v1

v2 whole, which is shorter than its diff:
```python
import functools

import jax
import jax.numpy as jnp
from jax import lax
from jax.experimental import pallas as pl
from jax.experimental.pallas import tpu as pltpu
from jax.sharding import PartitionSpec as P

EPS = 1e-05
ALPHA = 0.0625
LOSS_SCALE = 4096.0
AXES = ("grp", "tp", "tok")
F32 = jnp.float32
BF16 = jnp.bfloat16
VMEM_LIMIT = 16 * 1024 * 1024
WIDE_LIMIT = 20 * 1024 * 1024
NX, NY, NZ = 4, 4, 8
NTP = NX * NY
TOKENS = 256
KT = 512
KS = 128
VOC = 256


def permute(value, move):
    pairs = []
    for g in range(2):
        for x in range(NX):
            for y in range(NY):
                for z in range(NZ):
                    g2, x2, y2, z2 = move(g, x, y, z)
                    source = (g * NTP + x * NY + y) * NZ + z
                    target = ((g2 % 2) * NTP + (x2 % NX) * NY + y2 % NY) * NZ + z2 % NZ
                    pairs.append((source, target))
    return lax.ppermute(value, AXES, pairs)


def swap_cores(value):
    return permute(value, lambda g, x, y, z: (g + 1, x, y, z))


def shift_first(value, d):
    return permute(value, lambda g, x, y, z: (g, x, y + d, z) if g == 0 else (g, x + d, y, z))


def shift_second(value, d):
    return permute(value, lambda g, x, y, z: (g, x + d, y, z) if g == 0 else (g, x, y + d, z))


def params(limit=VMEM_LIMIT):
    return pltpu.CompilerParams(vmem_limit_bytes=limit)


def dot(a, b, dims):
    return lax.dot_general(a, b, (dims, ((), ())), preferred_element_type=F32)


def bring_kernel(w4, s4, w_own, s_own, sems):
    g = lax.axis_index("grp")
    copies = [
        pltpu.make_async_copy(source.at[:, g], target, sems.at[i])
        for i, (source, target) in enumerate(((w4, w_own), (s4, s_own)))
    ]
    for c in copies:
        c.start()
    for c in copies:
        c.wait()


def bring_halves(w4, s4):
    vmem = pl.BlockSpec(memory_space=pltpu.VMEM)
    hbm = pl.BlockSpec(memory_space=pl.ANY)
    return pl.pallas_call(
        bring_kernel,
        in_specs=[hbm, hbm],
        out_specs=[vmem, vmem],
        out_shape=[
            jax.ShapeDtypeStruct((NTP, KT, VOC), BF16),
            jax.ShapeDtypeStruct((NTP, KS, VOC), BF16),
        ],
        scratch_shapes=[pltpu.SemaphoreType.DMA((2,))],
        compiler_params=params(),
    )(w4, s4)


def logits_kernel(offsets, first, *refs):
    refs = list(refs)
    take = lambda n: [refs.pop(0) for _ in range(n)]
    arrays = 2 * len(offsets)
    hidden = take(arrays)
    r_t, r_s, gain_t, gain_s, w_own, w_oth, s_own, s_oth = take(8)
    before = None if first else take(3)[0]
    logits, normed_s, raw_s, acc, h_buf, w_buf, s_buf, n_buf, t_buf, in_sem, out_sem, acc_sem = refs
    g = lax.axis_index("grp")
    tp = lax.axis_index("tp")
    x, y = lax.div(tp, NY), lax.rem(tp, NY)
    position, line = jnp.where(g == 0, x, y), jnp.where(g == 0, y, x)
    copy = pltpu.make_async_copy
    if not first:
        load = copy(before, acc, acc_sem)
        load.start()
    places, arriving, leaving = [], [], []
    for a in range(arrays):
        ahead = lax.rem(position + offsets[a // 2] + NX, NX)
        for k in range(2):
            order = lax.rem(line - (2 * (a % 2) + k) + NX, NX)
            place = jnp.where(g == 0, ahead * NY + order, order * NY + ahead)
            places.append(place)
            t_rows, s_rows = pl.ds(k * KT, KT), pl.ds(k * KS, KS)
            sources = (
                (hidden[a].at[k], h_buf.at[a, k]),
                (w_own.at[place], w_buf.at[a, 0, t_rows]),
                (w_oth.at[place, g], w_buf.at[a, 1, t_rows]),
                (s_own.at[place], s_buf.at[a, 0, s_rows]),
                (s_oth.at[place, g], s_buf.at[a, 1, s_rows]),
            )
            n = 2 * a + k
            arriving.append([copy(p, q, in_sem.at[n, i]) for i, (p, q) in enumerate(sources)])
            for c in arriving[n]:
                c.start()
    for a in range(arrays):
        for k in range(2):
            n = 2 * a + k
            place = places[n]
            for c in arriving[n]:
                c.wait()
            row = pl.ds(place * 2 + g, 1)
            h_t = h_buf[a, k, :, :KT].astype(F32)
            t_buf[a, :, k * KT : (k + 1) * KT] = (h_t * r_t[...] * gain_t[row, :]).astype(BF16)
            h_s = h_buf[a, k, :, KT:].astype(F32)
            n_buf[a, :, k * KS : (k + 1) * KS] = (h_s * r_s[...] * gain_s[row, :]).astype(BF16)
            pairs = (
                (n_buf.at[a, :, pl.ds(k * KS, KS)], normed_s.at[place]),
                (h_buf.at[a, k, :, pl.ds(KT, KS)], raw_s.at[place]),
            )
            leaving.append([copy(p, q, out_sem.at[n, i]) for i, (p, q) in enumerate(pairs)])
            for c in leaving[n]:
                c.start()
        if a == 0 and not first:
            load.wait()
        nn = ((1,), (0,))
        for i, c in ((0, g), (1, 1 - g)):
            t = dot(t_buf[a], w_buf[a, i], nn)
            s = dot(n_buf[a], s_buf[a, i], nn)
            if a == 0 and first:
                acc[c, 0] = t
                acc[c, 1] = s
            else:
                acc[c, 0] += t
                acc[c, 1] += s
    store = copy(acc, logits, acc_sem)
    store.start()
    for copies in leaving:
        for c in copies:
            c.wait()
    store.wait()


def partial_logits(offsets, hidden, scales, gains, weights, before):
    first = before is None
    arrays = 2 * len(offsets)
    vmem = pl.BlockSpec(memory_space=pltpu.VMEM)
    hbm = pl.BlockSpec(memory_space=pl.ANY)
    out = pl.BlockSpec(memory_space=pltpu.HBM)
    operands = [*hidden, *scales, *gains, *weights]
    in_specs = [*[hbm] * arrays, *[vmem] * 4, *[hbm] * 4]
    aliases = {}
    if not first:
        aliases = {len(operands) + 1: 1, len(operands) + 2: 2}
        operands += before
        in_specs += [out] * 3
    return pl.pallas_call(
        functools.partial(logits_kernel, offsets, first),
        in_specs=in_specs,
        out_specs=[out] * 3,
        out_shape=[
            jax.ShapeDtypeStruct((2, 2, TOKENS, VOC), F32),
            jax.ShapeDtypeStruct((NTP, TOKENS, KS), BF16),
            jax.ShapeDtypeStruct((NTP, TOKENS, KS), BF16),
        ],
        scratch_shapes=[
            pltpu.VMEM((2, 2, TOKENS, VOC), F32),
            pltpu.VMEM((arrays, 2, TOKENS, KT + KS), BF16),
            pltpu.VMEM((arrays, 2, 2 * KT, VOC), BF16),
            pltpu.VMEM((arrays, 2, 2 * KS, VOC), BF16),
            pltpu.VMEM((arrays, TOKENS, 2 * KS), BF16),
            pltpu.VMEM((arrays, TOKENS, 2 * KT), BF16),
            pltpu.SemaphoreType.DMA((2 * arrays, 5)),
            pltpu.SemaphoreType.DMA((2 * arrays, 2)),
            pltpu.SemaphoreType.DMA,
        ],
        input_output_aliases=aliases,
        cost_estimate=pl.CostEstimate(
            flops=4 * arrays * TOKENS * 2 * VOC * (KT + KS),
            bytes_accessed=arrays * 2_400_000,
            transcendentals=0,
        ),
        compiler_params=params(WIDE_LIMIT),
    )(*operands)


def onehot_of(targets, base):
    spread = jnp.broadcast_to(targets.astype(F32), (128, TOKENS))
    targets = jnp.transpose(spread)[:, 0:1].astype(jnp.int32)
    lane = lax.broadcasted_iota(jnp.int32, (TOKENS, 2 * VOC), 1)
    column = jnp.where(lane < VOC, base[0] + lane, base[1] + lane - VOC)
    return column == targets


def stats_kernel(base, mine, other, targets, both, records):
    t, s = (
        jnp.concatenate([mine[0, i] + other[0, i], mine[1, i] + other[1, i]], axis=1)
        for i in range(2)
    )
    both[0] = t
    both[1] = s

    def row_sum(v):
        return jnp.sum(v, axis=1, keepdims=True)

    m_t = jnp.max(t, axis=1, keepdims=True)
    m_s = jnp.max(s, axis=1, keepdims=True)
    e_t = jnp.exp(t - m_t)
    hit = onehot_of(targets[...], base)
    columns = [
        m_t, row_sum(e_t), row_sum(e_t * (t - s)), m_s, row_sum(jnp.exp(s - m_s)),
        row_sum(jnp.where(hit, s, 0.0)),
    ]
    lane = lax.broadcasted_iota(jnp.int32, (TOKENS, 128), 1)
    packed = jnp.zeros((TOKENS, 128), F32)
    for k, column in enumerate(columns):
        packed = jnp.where(lane == k, column, packed)
    rows = jnp.transpose(packed)[:8]
    for k in range(NTP):
        records[k] = rows


def local_stats(base, mine, other, targets):
    vmem = pl.BlockSpec(memory_space=pltpu.VMEM)
    return pl.pallas_call(
        stats_kernel,
        in_specs=[pl.BlockSpec(memory_space=pltpu.SMEM), vmem, vmem, vmem],
        out_specs=[vmem, vmem],
        out_shape=[
            jax.ShapeDtypeStruct((2, TOKENS, 2 * VOC), F32),
            jax.ShapeDtypeStruct((NTP, 8, TOKENS), F32),
        ],
        compiler_params=params(),
    )(base, mine, other, targets)


def merged(records):
    m_t, z_t, a, m_s, z_s, hit = (records[:, k, :] for k in range(6))
    top_t = jnp.max(m_t, axis=0, keepdims=True)
    top_s = jnp.max(m_s, axis=0, keepdims=True)
    w_t = jnp.exp(m_t - top_t)
    w_s = jnp.exp(m_s - top_s)

    def total(v):
        return jnp.sum(v, axis=0, keepdims=True)

    return top_t, total(w_t * z_t), total(w_t * a), top_s, total(w_s * z_s), total(hit)


def merge_kernel(copies, records, out):
    rows = merged(records[...])
    for c in range(copies):
        for k in range(6):
            out[c, k : k + 1, :] = rows[k]
        out[c, 6:8, :] = jnp.zeros((2, TOKENS), F32)


def merge_records(records, copies):
    vmem = pl.BlockSpec(memory_space=pltpu.VMEM)
    return pl.pallas_call(
        functools.partial(merge_kernel, copies),
        in_specs=[vmem],
        out_specs=vmem,
        out_shape=jax.ShapeDtypeStruct((copies, 8, TOKENS), F32),
        compiler_params=params(),
    )(records)


def grad_kernel(
    base, records, both, targets, r_s, raw_s, s_own, s_oth, out, grad_own, loss, grads, gains, parts, sems
):
    j = pl.program_id(0)
    g = base[2]

    @pl.when(j == 0)
    def _():
        top_t, z_t, a, top_s, z_s, hit = merged(records[...])
        lse_t = top_t + jnp.log(z_t)
        lse_s = top_s + jnp.log(z_s)
        loss[...] = a / z_t - lse_t + lse_s + ALPHA * (lse_s - hit)
        row = lax.broadcasted_iota(jnp.int32, (128, TOKENS), 0)
        packed = jnp.where(row == 0, lse_t, jnp.where(row == 1, lse_s, 0.0))
        columns = jnp.transpose(packed)
        p_t = jnp.exp(both[0] - columns[:, 0:1])
        p_s = jnp.exp(both[1] - columns[:, 1:2])
        hits = onehot_of(targets[...], base).astype(F32)
        grad = (LOSS_SCALE * ((1.0 + ALPHA) * p_s - p_t - ALPHA * hits)).astype(BF16)
        grads[0] = grad[:, :VOC]
        grads[1] = grad[:, VOC:]
        grad_own[...] = grads[g]

    nt = ((1,), (1,))
    wide = (4 * KS, VOC)
    part = dot(grads[g], s_own[...].reshape(wide), nt) + dot(grads[1 - g], s_oth[...].reshape(wide), nt)
    for k in range(4):
        piece = part[:, k * KS : (k + 1) * KS]
        rows = pl.ds(pl.multiple_of((j * 4 + k) * 16, 16), 16)
        parts[:, rows, :] = piece.astype(BF16).reshape(NTP, 16, KS)
        xhat = raw_s[k].astype(F32) * r_s[...]
        gains[pl.ds(j * 4 + k, 1), :] = jnp.sum(piece * xhat, axis=0, keepdims=True)

    def leave(n, count):
        rows = pl.ds(pl.multiple_of(n * 64, 64), count)
        return pltpu.make_async_copy(parts.at[:, rows, :], out.at[:, rows, :], sems.at[n])

    leave(j, 64).start()

    @pl.when(j == 3)
    def _():
        gain = gains[...]
        high = gain.astype(BF16)
        low = (gain - high.astype(F32)).astype(BF16)
        for c in range(NTP):
            parts[c, 256:272, :] = high
            parts[c, 272:288, :] = low
        leave(4, 32).start()
        for n in range(4):
            leave(n, 64).wait()
        leave(4, 32).wait()


def grad_parts(base, records, both, targets, r_s, raw_s, s_own, s_oth):
    whole = lambda *shape: pl.BlockSpec(shape, lambda j, b: (0,) * len(shape))
    grid_spec = pltpu.PrefetchScalarGridSpec(
        num_scalar_prefetch=1,
        grid=(4,),
        in_specs=[
            whole(NZ, 8, TOKENS), whole(2, TOKENS, 2 * VOC), whole(1, TOKENS), whole(TOKENS, 1),
            pl.BlockSpec((4, TOKENS, KS), lambda j, b: (j, 0, 0)),
            pl.BlockSpec((4, KS, VOC), lambda j, b: (j, 0, 0)),
            pl.BlockSpec((4, 1, KS, VOC), lambda j, b: (j, b[2], 0, 0)),
        ],
        out_specs=[
            pl.BlockSpec(memory_space=pltpu.HBM), whole(TOKENS, VOC), whole(1, TOKENS),
        ],
        scratch_shapes=[
            pltpu.VMEM((2, TOKENS, VOC), BF16),
            pltpu.VMEM((NTP, KS), F32),
            pltpu.VMEM((NTP, 288, KS), BF16),
            pltpu.SemaphoreType.DMA((5,)),
        ],
    )
    return pl.pallas_call(
        grad_kernel,
        grid_spec=grid_spec,
        out_shape=[
            jax.ShapeDtypeStruct((NTP, 288, KS), BF16),
            jax.ShapeDtypeStruct((TOKENS, VOC), BF16),
            jax.ShapeDtypeStruct((1, TOKENS), F32),
        ],
        compiler_params=params(),
    )(base, records, both, targets, r_s, raw_s, s_own, s_oth)


def head_kernel(base, mine, other, grad, out):
    g = base[2]
    tn = ((0,), (0,))
    for k in range(4):
        out[k, g] = dot(mine[k], grad[...], tn).astype(BF16)
        out[k, 1 - g] = dot(other[k], grad[...], tn).astype(BF16)


def head_gradient(base, mine, other, grad):
    block = pl.BlockSpec((4, TOKENS, KS), lambda j, b: (j, 0, 0))
    grid_spec = pltpu.PrefetchScalarGridSpec(
        num_scalar_prefetch=1,
        grid=(4,),
        in_specs=[block, block, pl.BlockSpec((TOKENS, VOC), lambda j, b: (0, 0))],
        out_specs=pl.BlockSpec((4, 2, KS, VOC), lambda j, b: (j, 0, 0, 0)),
    )
    return pl.pallas_call(
        head_kernel,
        grid_spec=grid_spec,
        out_shape=jax.ShapeDtypeStruct((NTP, 2, KS, VOC), BF16),
        cost_estimate=pl.CostEstimate(
            flops=2 * NTP * 2 * KS * TOKENS * VOC, bytes_accessed=4_500_000, transcendentals=0
        ),
        compiler_params=params(),
    )(base, mine, other, grad)


def fold_kernel(parts, out, total):
    acc = parts[0].astype(F32)
    for k in range(1, NTP):
        acc = acc + parts[k].astype(F32)
    total[...] = acc
    gain = total[256:272, :] + total[272:288, :]
    for z in range(NZ):
        for i in range(2):
            out[z, i * 16 : (i + 1) * 16, :] = total[pl.ds(2 * z + i, 16, stride=16), :]
        out[z, 32:48, :] = gain


def fold_parts(parts):
    vmem = pl.BlockSpec(memory_space=pltpu.VMEM)
    return pl.pallas_call(
        fold_kernel,
        in_specs=[vmem],
        out_specs=vmem,
        out_shape=jax.ShapeDtypeStruct((NZ, 48, KS), F32),
        scratch_shapes=[pltpu.VMEM((288, KS), F32)],
        compiler_params=params(),
    )(parts)


def sum_kernel(parts, rows, out):
    acc = parts[0]
    for k in range(1, NZ):
        acc = acc + parts[k]
    out[0:48, :] = acc
    out[48:80, :] = rows[...]


def sum_parts(parts, rows):
    vmem = pl.BlockSpec(memory_space=pltpu.VMEM)
    return pl.pallas_call(
        sum_kernel,
        in_specs=[vmem, vmem],
        out_specs=vmem,
        out_shape=jax.ShapeDtypeStruct((80, KS), F32),
        compiler_params=params(),
    )(parts, rows)


def final_kernel(mine, other, gain, hidden, gain_gradient, rows):
    g = lax.axis_index("grp")

    def all_features(v):
        return jnp.sum(v)

    halves = (mine, other)
    total = []
    for i in range(2):
        own_rows = slice(48 + 16 * i, 64 + 16 * i)
        squares = sum(all_features(h[own_rows, :] * h[own_rows, :]) for h in halves)
        scale = lax.rsqrt(jnp.full((1, 1), squares / (2 * NTP * KS) + EPS, F32))
        pairs = []
        for k, h in enumerate(halves):
            xhat = h[own_rows, :] * scale
            dy = h[16 * i : 16 * i + 16, :] * gain[g if k == 0 else 1 - g]
            pairs.append((xhat, dy))
        mean = sum(all_features(dy * xhat) for xhat, dy in pairs) / (2 * NTP * KS)
        total.append([scale * (dy - xhat * mean) for xhat, dy in pairs])
    for k, h in enumerate(halves):
        c = g if k == 0 else 1 - g
        for j in range(NTP):
            lanes = pl.ds(pl.multiple_of((2 * j + c) * KS, KS), KS)
            for i in range(2):
                rows[i : i + 1, lanes] = total[i][k][j : j + 1, :]
            gain_gradient[:, lanes] = h[32 + j : 33 + j, :]
    hidden[...] = rows[0:2, :].astype(BF16)


def norm_backward(mine, other, gain):
    vmem = pl.BlockSpec(memory_space=pltpu.VMEM)
    return pl.pallas_call(
        final_kernel,
        in_specs=[vmem] * 3,
        out_specs=[vmem] * 2,
        out_shape=[
            jax.ShapeDtypeStruct((2, 2 * NTP * KS), BF16),
            jax.ShapeDtypeStruct((1, 2 * NTP * KS), F32),
        ],
        scratch_shapes=[pltpu.VMEM((8, 2 * NTP * KS), F32)],
        compiler_params=params(),
    )(mine, other, gain)


def squares_kernel(slab, out):
    def lanes(low, high):
        total = 0.0
        for k in range(low, high, 128):
            v = slab[:, k : k + 128].astype(F32)
            total = total + v * v
        return jnp.sum(jnp.transpose(total), axis=0, keepdims=True)

    out[0:1, :] = lanes(0, KT)
    out[1:2, :] = lanes(KT, KT + KS)
    out[2:8, :] = jnp.zeros((6, TOKENS), F32)


def both_kernel(mine, other, out):
    total = mine[...] + other[...]
    for k in range(NTP):
        out[k] = total


def scales_kernel(widths, squares, r_t, r_s):
    total = jnp.sum(squares[...], axis=0)
    columns = jnp.transpose(
        jnp.concatenate(
            [lax.rsqrt(total[i : i + 1, :] / widths[i] + EPS) for i in range(2)]
            + [jnp.zeros((126, TOKENS), F32)],
            axis=0,
        )
    )
    r_t[...] = columns[:, 0:1]
    r_s[...] = columns[:, 1:2]


def small_call(kernel, shapes, *operands):
    vmem = pl.BlockSpec(memory_space=pltpu.VMEM)
    return pl.pallas_call(
        kernel,
        in_specs=[vmem] * len(operands),
        out_specs=[vmem] * len(shapes),
        out_shape=[jax.ShapeDtypeStruct(shape, F32) for shape in shapes],
        compiler_params=params(),
    )(*operands)


def on_device(
    teacher_hidden, teacher_gain, teacher_head, student_hidden, student_gain, student_head, targets
):
    g = lax.axis_index("grp")
    tp = lax.axis_index("tp")
    z = lax.axis_index("tok")

    w4 = teacher_head.reshape(NTP, 2, KT, VOC)
    s4 = student_head.reshape(NTP, 2, KS, VOC)
    w_oth, s_oth = swap_cores(w4), swap_cores(s4)

    block = jnp.concatenate(
        [
            lax.dynamic_slice_in_dim(teacher_hidden, g * KT, KT, 1),
            lax.dynamic_slice_in_dim(student_hidden, g * KS, KS, 1),
        ],
        axis=1,
    )
    slab = lax.all_to_all(
        jnp.broadcast_to(block[None], (NZ, *block.shape)), "tok", 0, 0, tiled=True
    ).reshape(TOKENS, KT + KS)
    w_own, s_own = bring_halves(w4, s4)
    gain_t, gain_s = teacher_gain.reshape(32, KT), student_gain.reshape(32, KS)
    slab, w_oth, s_oth, w_own, s_own, gain_t, gain_s = lax.optimization_barrier(
        (slab, w_oth, s_oth, w_own, s_own, gain_t, gain_s)
    )
    by_shift = [shift_first(slab, d) for d in (1, 2, 3)]
    (half,) = small_call(squares_kernel, [(8, TOKENS)], slab)
    (copies,) = small_call(both_kernel, [(NTP, 8, TOKENS)], half, swap_cores(half))
    widths = (teacher_gain.shape[0], student_gain.shape[0])
    r_t, r_s = small_call(
        functools.partial(scales_kernel, widths),
        [(TOKENS, 1), (TOKENS, 1)],
        lax.all_to_all(copies, "tp", 0, 0, tiled=True),
    )
    low, high = jnp.stack([slab, by_shift[0]]), jnp.stack(by_shift[1:])
    low, high, r_t, r_s = lax.optimization_barrier((low, high, r_t, r_s))
    back_low = shift_second(low, 1)
    fore_high = shift_second(high, -1)
    back_high = shift_second(high, 1)
    fore_low = shift_second(low, -1)
    heads = functools.partial(
        partial_logits,
        scales=(r_t, r_s),
        gains=(gain_t, gain_s),
        weights=(w_own, w_oth, s_own, s_oth),
    )
    done = heads((0,), (low, high), before=None)
    *done, back_low, fore_high = lax.optimization_barrier((*done, back_low, fore_high))
    far_low = shift_second(back_low, 1)
    far_high = shift_second(fore_high, -1)
    done = heads((-1, 1), (back_low, back_high, fore_low, fore_high), before=done)
    half, normed_s, raw_s = heads((2,), (far_low, far_high), before=done)
    column = (tp * NZ + z) * VOC
    base = jnp.stack([column, NTP * NZ * VOC + column, g]).astype(jnp.int32)
    targets_row = targets[None, :]
    both, records = local_stats(base, half, swap_cores(half), targets_row)
    normed_oth = swap_cores(normed_s)
    records, normed_oth = lax.optimization_barrier((records, normed_oth))
    records = lax.all_to_all(records, "tp", 0, 0, tiled=True)
    records = lax.all_to_all(merge_records(records, NZ), "tok", 0, 0, tiled=True)
    parts, grad_own, loss = grad_parts(
        base, records, both, targets_row, r_s, raw_s, s_own, s_oth
    )
    arrived = lax.all_to_all(parts, "tp", 0, 0, tiled=True)
    d_head = head_gradient(base, normed_s, normed_oth, grad_own)
    arrived, d_head = lax.optimization_barrier((arrived, d_head))
    arrived = lax.all_to_all(fold_parts(arrived), "tok", 0, 0, tiled=True)
    hidden_rows = lax.dynamic_slice_in_dim(raw_s, tp * 16 + z * 2, 2, 1)
    hidden_rows = hidden_rows.astype(F32).transpose(1, 0, 2).reshape(32, KS)
    mine = sum_parts(arrived, hidden_rows)
    hidden_gradient, gain_gradient = norm_backward(
        mine, swap_cores(mine), student_gain.reshape(NTP, 2, KS).transpose(1, 0, 2)
    )
    return (
        loss.reshape(TOKENS),
        d_head.reshape(student_head.shape),
        hidden_gradient,
        gain_gradient.reshape(2 * NTP * KS),
    )


def solution(mesh):
    placed = (
        P("tok", "tp"),
        P(),
        P(None, ("grp", "tp", "tok")),
        P("tok", "tp"),
        P(),
        P(None, ("grp", "tp", "tok")),
        P(),
    )
    return jax.shard_map(
        on_device,
        mesh=mesh,
        in_specs=placed,
        out_specs=(P(), P(None, ("grp", "tp", "tok")), P(("tp", "tok"), None), P()),
        check_vma=False,
    )
```

time: 173 us -> 149 us (0.86)
  starting transfers between devices: 57.3 us -> 38.3 us
  blocking collectives: 21.1 us -> 33.8 us
  waiting for transfers between devices: 43.2 us -> 32.2 us
  other arithmetic: 8.91 us -> 1 us
  local copies, waits for them, and re-layouts: 12.2 us -> 14.2 us
    ppermute x20 -> x15, starting transfers between devices: 50.1 us -> 24.8 us  [permute(): return lax.ppermute(value, AXES, pairs)]
    ppermute x20 -> x15, waiting for transfers between devices: 21.8 us -> 9.13 us  [permute(): return lax.ppermute(value, AXES, pairs)]
    all_to_all x0 -> x1, blocking collectives: none -> 12.3 us  [on_device(): lax.all_to_all(copies, 'tp', 0, 0, tiled=True)]
    unnamed x39 -> x26, local copies, waits for them, and re-layouts: 2.23 us -> 11.2 us
    reduce_sum x12 -> x0, other arithmetic: 6.51 us -> none  [the longest x10 6.23 us: squares(): total = total + jnp.sum(v * v, axis=(0, 2))]
    all_to_all x1 -> x2, starting transfers between devices: 3.83 us -> 10.1 us  [the longest x1 6.45 us: on_device(): lax.all_to_all(jnp.broadcast_to(block[None], (NZ, *block.shape)), 'tok',...]
    squeeze x2 -> x0, local copies, waits for them, and re-layouts: 5.62 us -> none  [the longest x1 4.54 us: on_device(): w_oth = swap_cores(lax.dynamic_index_in_dim(w4, 1 - g, 1, keepdims=False))]
    all_to_all x1, blocking collectives: 9.31 us -> 11.8 us  [on_device(): records = lax.all_to_all(records, 'tp', 0, 0, tiled=True)]
  transfers between devices with their start and end apart: 22 -> 18, of which waited for: 11 -> 9; matrix products, arithmetic and copies ran while one was open for 9% -> 3% of each run, Pallas kernels for 3% -> 12%
where the time goes in v2:
time: 149 us; the launch traced here: 148 us
  starting transfers between devices  38.3 us (26%)
  blocking collectives  33.8 us (23%)
  waiting for transfers between devices  32.2 us (22%)
  Pallas kernels  27.4 us (18%)
  local copies, waits for them, and re-layouts  14.2 us (10%)
    ppermute x15, starting transfers between devices, permute(): return lax.ppermute(value, AXES, pairs)  24.8 us
    pallas_call x3, Pallas kernels, partial_logits(): pl.pallas_call(functools.partial(logits_kernel, offsets, first), in_specs...  14.1 us
    all_to_all x1, blocking collectives, on_device(): lax.all_to_all(copies, 'tp', 0, 0, tiled=True)  12.3 us
    all_to_all x1, blocking collectives, on_device(): records = lax.all_to_all(records, 'tp', 0, 0, tiled=True)  11.8 us
    unnamed x26, local copies, waits for them, and re-layouts  11.2 us
    all_to_all x1, waiting for transfers between devices, on_device(): arrived = lax.all_to_all(parts, 'tp', 0, 0, tiled=True)  10.9 us
    all_to_all x1, blocking collectives, on_device(): lax.all_to_all(merge_records(records, NZ), 'tok', 0, 0, tiled=True)  9.71 us
    ppermute x15, waiting for transfers between devices, permute(): return lax.ppermute(value, AXES, pairs)  9.13 us
  transfers between devices with their start and end apart: 18, of which 9 were waited for; matrix products, arithmetic and copies ran while one was open for 3% of the time, Pallas kernels for 12%

profile of v2, /device:TPU:1, one launch (start us, length us, event | category | flops | bytes accessed | tf_op | source)
XLA Modules:
  0.0 147.7 jit_solution(7121237348785517738)
XLA Ops:
  0.6 3.3 %collective-permute-start = (bf16[16,2,512,256]{3,2,1,0:T(8,128)(2,1)}, bf16[16,2,512,256]{3,2,1,0:T(8,128)(2,1)}, u32[]{:S(2)}, u32[]{:S(2)}) collective-permute-start(bf16[16,2,512,256]{3,2,1,0:T(8,128)(2,1)} %bitcast.22), channel_id=1, source_target_pairs={{0,128},{1,129},{2,130},{3,131},{4,132},{5,133},{6,134},{7,135},{8... | collective-permute-start | bytes 25165832 | tf_op jit(solution)/shard_map/ppermute | solution.py:36
  5.5 6.5 %all-to-all-start = ((bf16[8,32,640]{2,1,0:T(8,128)(2,1)}), bf16[8,32,640]{2,1,0:T(8,128)(2,1)S(1)}, u32[]{:S(2)}, u32[]{:S(2)}) async-start(bf16[8,32,640]{2,1,0:T(8,128)(2,1)} %broadcast_in_dim.4), calls=%async_computation | async-start | bytes 655360 | tf_op jit(solution)/shard_map/all_to_all | solution.py:546
  12.0 3.4 %copy-done.5 = bf16[16384,256]{1,0:T(8,128)(2,1)S(1)} copy-done((bf16[16384,256]{1,0:T(8,128)(2,1)S(1)}, bf16[16384,256]{1,0:T(8,128)(2,1)}, u32[]{:S(2)}) %copy-start.5) | copy-done | bytes 8388632
  20.8 4.4 %all-to-all-done = bf16[8,32,640]{2,1,0:T(8,128)(2,1)S(1)} async-done(((bf16[8,32,640]{2,1,0:T(8,128)(2,1)}), bf16[8,32,640]{2,1,0:T(8,128)(2,1)S(1)}, u32[]{:S(2)}, u32[]{:S(2)}) %all-to-all-start) | async-done | bytes 327712 | tf_op jit(solution)/shard_map/all_to_all | solution.py:546
  25.3 2.6 %collective-permute-start.4 = (bf16[256,640]{1,0:T(8,128)(2,1)S(1)}, bf16[256,640]{1,0:T(8,128)(2,1)S(1)}, u32[]{:S(2)}, u32[]{:S(2)}) collective-permute-start(bf16[256,640]{1,0:T(8,128)(2,1)S(1)} %bitcast.24), channel_id=1, source_target_pairs={{0,24},{1,25},{2,26},{3,27},{4,28},{5,29},{6,30},{7,31},{8,0},{9,1... | collective-permute-start | bytes 983048 | tf_op jit(solution)/shard_map/ppermute | solution.py:36
  32.0 12.3 %all_to_all.30.squares = f32[16,8,256]{2,1,0:T(8,128)S(1)} all-to-all(f32[16,8,256]{2,1,0:T(8,128)S(1)} %shard_map.104), channel_id=1, replica_groups=mesh['grp'=2,'tp'=16,'tok'=8] {'tp'}, dimensions={0} | all-to-all | bytes 262144 | tf_op jit(solution)/shard_map/all_to_all | solution.py:561
  45.1 2.5 %collective-permute-start.7 = (bf16[2,256,640]{2,1,0:T(8,128)(2,1)S(1)}, bf16[2,256,640]{2,1,0:T(8,128)(2,1)S(1)}, u32[]{:S(2)}, u32[]{:S(2)}) collective-permute-start(bf16[2,256,640]{2,1,0:T(8,128)(2,1)S(1)} %pad_maximum_fusion.1.refs_1_), channel_id=1, source_target_pairs={{0,96},{1,97},{2,98},{3,99},{4,100},{5,101},{6,102},{7,103},{8,104... | collective-permute-start | bytes 1966088 | tf_op jit(solution)/shard_map/ppermute | solution.py:36
  47.6 2.7 %collective-permute-start.11 = (bf16[2,256,640]{2,1,0:T(8,128)(2,1)S(1)}, bf16[2,256,640]{2,1,0:T(8,128)(2,1)S(1)}, u32[]{:S(2)}, u32[]{:S(2)}) collective-permute-start(bf16[2,256,640]{2,1,0:T(8,128)(2,1)S(1)} %pad_maximum_fusion.refs_0_), channel_id=1, source_target_pairs={{0,96},{1,97},{2,98},{3,99},{4,100},{5,101},{6,102},{7,103},{8,104... | collective-permute-start | bytes 1966088 | tf_op jit(solution)/shard_map/ppermute | solution.py:36
  52.4 3.3 %shard_map.106 = (f32[2,2,256,256]{3,2,1,0:T(8,128)S(1)}, bf16[16,256,128]{2,1,0:T(8,128)(2,1)}, bf16[16,256,128]{2,1,0:T(8,128)(2,1)S(1)}) custom-call(bf16[2,256,640]{2,1,0:T(8,128)(2,1)S(1)} %pad_maximum_fusion.refs_0_, bf16[2,256,640]{2,1,0:T(8,128)(2,1)S(1)} %pad_maximum_fusion.1.refs_1_, f32[256,1]{1,0:T(8,128)S(1)} %get-tuple-element.51.refs_2_.refs_4_, ...), custom_call_target="tpu_custom_call" | custom-call | flops 671088640 | bytes 4800000 | tf_op jit(solution)/shard_map/pallas_call | solution.py:173
  55.8 2.7 %collective-permute-start.9 = (bf16[2,256,640]{2,1,0:T(8,128)(2,1)S(1)}, bf16[2,256,640]{2,1,0:T(8,128)(2,1)S(1)}, u32[]{:S(2)}, u32[]{:S(2)}) collective-permute-start(bf16[2,256,640]{2,1,0:T(8,128)(2,1)S(1)} %collective-permute-done.7.refs_3_), channel_id=1, source_target_pairs={{0,96},{1,97},{2,98},{3,99},{4,100},{5,101},{6,102},{7,103},{8,104... | collective-permute-start | bytes 1966088 | tf_op jit(solution)/shard_map/ppermute | solution.py:36
  58.5 4.3 %collective-permute-done.10.refs_1_ = bf16[2,256,640]{2,1,0:T(8,128)(2,1)S(1)} collective-permute-done((bf16[2,256,640]{2,1,0:T(8,128)(2,1)S(1)}, bf16[2,256,640]{2,1,0:T(8,128)(2,1)S(1)}, u32[]{:S(2)}, u32[]{:S(2)}) %collective-permute-start.10) | collective-permute-done | bytes 655392 | tf_op jit(solution)/shard_map/ppermute | solution.py:36
  62.8 6.6 %shard_map.107 = (f32[2,2,256,256]{3,2,1,0:T(8,128)S(1)}, bf16[16,256,128]{2,1,0:T(8,128)(2,1)}, bf16[16,256,128]{2,1,0:T(8,128)(2,1)S(1)}) custom-call(bf16[2,256,640]{2,1,0:T(8,128)(2,1)S(1)} %collective-permute-done.6.refs_0_, bf16[2,256,640]{2,1,0:T(8,128)(2,1)S(1)} %collective-permute-done.10.refs_1_, ...), custom_call_target="tpu_custom_call", output_to_operand_aliasing={{1}: (13, {}), {2}: (14, {})} | custom-call | flops 1342177280 | bytes 9600000 | tf_op jit(solution)/shard_map/pallas_call | solution.py:173
  69.9 4.2 %shard_map.108 = (f32[2,2,256,256]{3,2,1,0:T(8,128)}, bf16[16,256,128]{2,1,0:T(8,128)(2,1)}, bf16[16,256,128]{2,1,0:T(8,128)(2,1)S(1)}) custom-call(bf16[2,256,640]{2,1,0:T(8,128)(2,1)S(1)} %collective-permute-done.8.refs_0_, bf16[2,256,640]{2,1,0:T(8,128)(2,1)S(1)} %collective-permute-done.9.refs_1_, ...), custom_call_target="tpu_custom_call", output_to_operand_aliasing={{1}: (11, {}), {2}: (12, {})} | custom-call | flops 671088640 | bytes 4800000 | tf_op jit(solution)/shard_map/pallas_call | solution.py:173
  75.1 2.6 %collective-permute-start.12 = (f32[2,2,256,256]{3,2,1,0:T(8,128)}, f32[2,2,256,256]{3,2,1,0:T(8,128)}, u32[]{:S(2)}, u32[]{:S(2)}) collective-permute-start(f32[2,2,256,256]{3,2,1,0:T(8,128)} %get-tuple-element.70.mine), channel_id=1, source_target_pairs={{0,128},{1,129},{2,130},{3,131},{4,132},{5,133},{6,134},{7,135},{8... | collective-permute-start | bytes 3145736 | tf_op jit(solution)/shard_map/ppermute | solution.py:36
  77.8 2.5 %collective-permute-done.12.other = f32[2,2,256,256]{3,2,1,0:T(8,128)} collective-permute-done((f32[2,2,256,256]{3,2,1,0:T(8,128)}, f32[2,2,256,256]{3,2,1,0:T(8,128)}, u32[]{:S(2)}, u32[]{:S(2)}) %collective-permute-start.12) | collective-permute-done | bytes 1048608 | tf_op jit(solution)/shard_map/ppermute | solution.py:36
  82.5 11.8 %all_to_all.31.records = f32[16,8,256]{2,1,0:T(8,128)S(1)} all-to-all(f32[16,8,256]{2,1,0:T(8,128)S(1)} %get-tuple-element.73), channel_id=1, replica_groups=mesh['grp'=2,'tp'=16,'tok'=8] {'tp'}, dimensions={0} | all-to-all | bytes 262144 | tf_op jit(solution)/shard_map/all_to_all | solution.py:587
  94.4 9.7 %all_to_all.32.records = f32[8,8,256]{2,1,0:T(8,128)S(1)} all-to-all(f32[8,8,256]{2,1,0:T(8,128)S(1)} %shard_map.110), channel_id=1, replica_groups=mesh['grp'=2,'tp'=16,'tok'=8] {'tok'}, dimensions={0} | all-to-all | bytes 131072 | tf_op jit(solution)/shard_map/all_to_all | solution.py:588
  104.1 3.4 %shard_map.111 = (bf16[16,288,128]{2,1,0:T(8,128)(2,1)S(1)}, bf16[256,256]{1,0:T(8,128)(2,1)S(1)}, f32[1,256]{1,0:T(1,128)}) custom-call(s32[3]{0:T(128)S(1)} %pad_add_fusion.base, f32[8,8,256]{2,1,0:T(8,128)S(1)} %all_to_all.32.records, f32[2,256,512]{2,1,0:T(8,128)S(1)} %get-tuple-element.74.both, s32[1,256]{1,0:T(1,128)S(1)} %bitcast.38, ...), custom_call_target="tpu_custom_call" | custom-call | tf_op jit(solution)/shard_map/pallas_call | solution.py:359
  108.5 3.7 %all-to-all-start.4 = ((bf16[16,288,128]{2,1,0:T(8,128)(2,1)}), bf16[16,288,128]{2,1,0:T(8,128)(2,1)S(1)}, u32[]{:S(2)}, u32[]{:S(2)}) async-start(bf16[16,288,128]{2,1,0:T(8,128)(2,1)} %copy-done.9), calls=%async_computation.4 | async-start | bytes 2359296 | tf_op jit(solution)/shard_map/all_to_all | solution.py:592
  112.2 4.9 %shard_map.112 = bf16[16,2,128,256]{3,2,1,0:T(8,128)(2,1)} custom-call(s32[3]{0:T(128)S(1)} %pad_add_fusion.base, bf16[16,256,128]{2,1,0:T(8,128)(2,1)} %get-tuple-element.72.mine, bf16[16,256,128]{2,1,0:T(8,128)(2,1)} %collective-permute-done.13.other, bf16[256,256]{1,0:T(8,128)(2,1)S(1)} %get-tuple-element.79.grad), custom_call_target="tpu_custom_call" | custom-call | flops 536870912 | bytes 4500000 | tf_op jit(solution)/shard_map/pallas_call | solution.py:387
  117.1 10.9 %all-to-all-done.4.parts = bf16[16,288,128]{2,1,0:T(8,128)(2,1)S(1)} async-done(((bf16[16,288,128]{2,1,0:T(8,128)(2,1)}), bf16[16,288,128]{2,1,0:T(8,128)(2,1)S(1)}, u32[]{:S(2)}, u32[]{:S(2)}) %all-to-all-start.4) | async-done | bytes 1179680 | tf_op jit(solution)/shard_map/all_to_all | solution.py:592
  128.9 3.4 %all-to-all-start.5 = ((f32[8,48,128]{2,1,0:T(8,128)}), f32[8,48,128]{2,1,0:T(8,128)S(1)}, u32[]{:S(2)}, u32[]{:S(2)}) async-start(f32[8,48,128]{2,1,0:T(8,128)} %shard_map.113), calls=%async_computation.5 | async-start | bytes 393216 | tf_op jit(solution)/shard_map/all_to_all | solution.py:595
  133.1 7.8 %all-to-all-done.5.parts = f32[8,48,128]{2,1,0:T(8,128)S(1)} async-done(((f32[8,48,128]{2,1,0:T(8,128)}), f32[8,48,128]{2,1,0:T(8,128)S(1)}, u32[]{:S(2)}, u32[]{:S(2)}) %all-to-all-start.5) | async-done | bytes 196640 | tf_op jit(solution)/shard_map/all_to_all | solution.py:595
  140.8 4.9 %collective-permute-start.14 = (f32[80,128]{1,0:T(8,128)S(1)}, f32[80,128]{1,0:T(8,128)S(1)}, u32[]{:S(2)}, u32[]{:S(2)}) collective-permute-start(f32[80,128]{1,0:T(8,128)S(1)} %shard_map.114.mine), channel_id=1, source_target_pairs={{0,128},{1,129},{2,130},{3,131},{4,132},{5,133},{6,134},{7,135},{8... | collective-permute-start | bytes 122888 | tf_op jit(solution)/shard_map/ppermute | solution.py:36
  (66 shorter events, 22.5 us)
Async XLA Ops:
  0.6 24.6 %collective-permute-start = (bf16[16,2,512,256]{3,2,1,0:T(8,128)(2,1)}, bf16[16,2,512,256]{3,2,1,0:T(8,128)(2,1)}, u32[]{:S(2)}, u32[]{:S(2)}) collective-permute-start(bf16[16,2,512,256]{3,2,1,0:T(8,128)(2,1)} %bitcast.22), channel_id=1, source_target_pairs={{0,128},{1,129},{2,130},{3,131},{4,132},{5,133},{6,134},{7,135},{8... | collective-permute-start | bytes 25165832 | tf_op jit(solution)/shard_map/ppermute | solution.py:36
  4.0 21.3 %collective-permute-start.1 = (bf16[16,2,128,256]{3,2,1,0:T(8,128)(2,1)}, bf16[16,2,128,256]{3,2,1,0:T(8,128)(2,1)S(1)}, u32[]{:S(2)}, u32[]{:S(2)}) collective-permute-start(bf16[16,2,128,256]{3,2,1,0:T(8,128)(2,1)} %bitcast.29), channel_id=1, source_target_pairs={{0,128},{1,129},{2,130},{3,131},{4,132},{5,133},{6,134},{7,135},{8... | collective-permute-start | bytes 6291464 | tf_op jit(solution)/shard_map/ppermute | solution.py:36
  5.5 19.7 %all-to-all-start = ((bf16[8,32,640]{2,1,0:T(8,128)(2,1)}), bf16[8,32,640]{2,1,0:T(8,128)(2,1)S(1)}, u32[]{:S(2)}, u32[]{:S(2)}) async-start(bf16[8,32,640]{2,1,0:T(8,128)(2,1)} %broadcast_in_dim.4), calls=%async_computation | async-start | bytes 655360 | tf_op jit(solution)/shard_map/all_to_all | solution.py:546
  19.4 30.9 %copy-start.11 = (f32[4096]{0:T(1024)S(1)}, f32[4096]{0:T(1024)}, u32[]{:S(2)}) copy-start(f32[4096]{0:T(1024)} %param.11) | copy-start | bytes 49156
  25.3 25.0 %copy-start.10 = (f32[32,512]{1,0:T(8,128)S(1)}, f32[32,512]{1,0:T(8,128)}, u32[]{:S(2)}) copy-start(f32[32,512]{1,0:T(8,128)} %reshape.44.refs_4_.refs_6_) | copy-start | bytes 196612
  25.3 19.3 %collective-permute-start.4 = (bf16[256,640]{1,0:T(8,128)(2,1)S(1)}, bf16[256,640]{1,0:T(8,128)(2,1)S(1)}, u32[]{:S(2)}, u32[]{:S(2)}) collective-permute-start(bf16[256,640]{1,0:T(8,128)(2,1)S(1)} %bitcast.24), channel_id=1, source_target_pairs={{0,24},{1,25},{2,26},{3,27},{4,28},{5,29},{6,30},{7,31},{8,0},{9,1... | collective-permute-start | bytes 983048 | tf_op jit(solution)/shard_map/ppermute | solution.py:36
  27.9 16.8 %collective-permute-start.3 = (bf16[256,640]{1,0:T(8,128)(2,1)S(1)}, bf16[256,640]{1,0:T(8,128)(2,1)S(1)}, u32[]{:S(2)}, u32[]{:S(2)}) collective-permute-start(bf16[256,640]{1,0:T(8,128)(2,1)S(1)} %bitcast.25), channel_id=1, source_target_pairs={{0,16},{1,17},{2,18},{3,19},{4,20},{5,21},{6,22},{7,23},{8,24},{9,... | collective-permute-start | bytes 983048 | tf_op jit(solution)/shard_map/ppermute | solution.py:36
  28.4 16.3 %collective-permute-start.2 = (bf16[256,640]{1,0:T(8,128)(2,1)S(1)}, bf16[256,640]{1,0:T(8,128)(2,1)S(1)}, u32[]{:S(2)}, u32[]{:S(2)}) collective-permute-start(bf16[256,640]{1,0:T(8,128)(2,1)S(1)} %bitcast.26), channel_id=1, source_target_pairs={{0,8},{1,9},{2,10},{3,11},{4,12},{5,13},{6,14},{7,15},{8,16},{9,17... | collective-permute-start | bytes 983048 | tf_op jit(solution)/shard_map/ppermute | solution.py:36
  29.1 2.9 %collective-permute-start.5 = (f32[8,256]{1,0:T(8,128)S(1)}, f32[8,256]{1,0:T(8,128)S(1)}, u32[]{:S(2)}, u32[]{:S(2)}) collective-permute-start(f32[8,256]{1,0:T(8,128)S(1)} %shard_map.103.mine), channel_id=1, source_target_pairs={{0,128},{1,129},{2,130},{3,131},{4,132},{5,133},{6,134},{7,135},{8... | collective-permute-start | bytes 24584 | tf_op jit(solution)/shard_map/ppermute | solution.py:36
  44.6 25.3 %copy-start.6 = (f32[256,1]{1,0:T(8,128)}, f32[256,1]{1,0:T(8,128)S(1)}, u32[]{:S(2)}) copy-start(f32[256,1]{1,0:T(8,128)S(1)} %get-tuple-element.52.refs_3_.refs_5_.r_s) | copy-start | bytes 3076
  44.8 11.0 %collective-permute-start.6 = (bf16[2,256,640]{2,1,0:T(8,128)(2,1)S(1)}, bf16[2,256,640]{2,1,0:T(8,128)(2,1)S(1)}, u32[]{:S(2)}, u32[]{:S(2)}) collective-permute-start(bf16[2,256,640]{2,1,0:T(8,128)(2,1)S(1)} %pad_maximum_fusion.refs_0_), channel_id=1, source_target_pairs={{0,32},{1,33},{2,34},{3,35},{4,36},{5,37},{6,38},{7,39},{8,40},{9,... | collective-permute-start | bytes 1966088 | tf_op jit(solution)/shard_map/ppermute | solution.py:36
  45.1 10.7 %collective-permute-start.7 = (bf16[2,256,640]{2,1,0:T(8,128)(2,1)S(1)}, bf16[2,256,640]{2,1,0:T(8,128)(2,1)S(1)}, u32[]{:S(2)}, u32[]{:S(2)}) collective-permute-start(bf16[2,256,640]{2,1,0:T(8,128)(2,1)S(1)} %pad_maximum_fusion.1.refs_1_), channel_id=1, source_target_pairs={{0,96},{1,97},{2,98},{3,99},{4,100},{5,101},{6,102},{7,103},{8,104... | collective-permute-start | bytes 1966088 | tf_op jit(solution)/shard_map/ppermute | solution.py:36
  47.6 15.3 %collective-permute-start.10 = (bf16[2,256,640]{2,1,0:T(8,128)(2,1)S(1)}, bf16[2,256,640]{2,1,0:T(8,128)(2,1)S(1)}, u32[]{:S(2)}, u32[]{:S(2)}) collective-permute-start(bf16[2,256,640]{2,1,0:T(8,128)(2,1)S(1)} %pad_maximum_fusion.1.refs_1_), channel_id=1, source_target_pairs={{0,32},{1,33},{2,34},{3,35},{4,36},{5,37},{6,38},{7,39},{8,40},{9,... | collective-permute-start | bytes 1966088 | tf_op jit(solution)/shard_map/ppermute | solution.py:36
  47.6 15.3 %collective-permute-start.11 = (bf16[2,256,640]{2,1,0:T(8,128)(2,1)S(1)}, bf16[2,256,640]{2,1,0:T(8,128)(2,1)S(1)}, u32[]{:S(2)}, u32[]{:S(2)}) collective-permute-start(bf16[2,256,640]{2,1,0:T(8,128)(2,1)S(1)} %pad_maximum_fusion.refs_0_), channel_id=1, source_target_pairs={{0,96},{1,97},{2,98},{3,99},{4,100},{5,101},{6,102},{7,103},{8,104... | collective-permute-start | bytes 1966088 | tf_op jit(solution)/shard_map/ppermute | solution.py:36
  55.8 14.0 %collective-permute-start.8 = (bf16[2,256,640]{2,1,0:T(8,128)(2,1)S(1)}, bf16[2,256,640]{2,1,0:T(8,128)(2,1)S(1)}, u32[]{:S(2)}, u32[]{:S(2)}) collective-permute-start(bf16[2,256,640]{2,1,0:T(8,128)(2,1)S(1)} %collective-permute-done.6.refs_0_), channel_id=1, source_target_pairs={{0,32},{1,33},{2,34},{3,35},{4,36},{5,37},{6,38},{7,39},{8,40},{9,... | collective-permute-start | bytes 1966088 | tf_op jit(solution)/shard_map/ppermute | solution.py:36
  55.8 14.0 %collective-permute-start.9 = (bf16[2,256,640]{2,1,0:T(8,128)(2,1)S(1)}, bf16[2,256,640]{2,1,0:T(8,128)(2,1)S(1)}, u32[]{:S(2)}, u32[]{:S(2)}) collective-permute-start(bf16[2,256,640]{2,1,0:T(8,128)(2,1)S(1)} %collective-permute-done.7.refs_3_), channel_id=1, source_target_pairs={{0,96},{1,97},{2,98},{3,99},{4,100},{5,101},{6,102},{7,103},{8,104... | collective-permute-start | bytes 1966088 | tf_op jit(solution)/shard_map/ppermute | solution.py:36
  69.9 10.5 %copy-start.12 = (s32[256]{0:T(256)S(1)}, s32[256]{0:T(256)}, u32[]{:S(2)}) copy-start(s32[256]{0:T(256)} %param.13) | copy-start | bytes 3076
  75.1 29.0 %copy-start.7 = (f32[256,1]{1,0:T(8,128)S(1)}, f32[256,1]{1,0:T(8,128)}, u32[]{:S(2)}) copy-start(f32[256,1]{1,0:T(8,128)} %copy-done.6) | copy-start | bytes 3076
  75.1 5.3 %collective-permute-start.12 = (f32[2,2,256,256]{3,2,1,0:T(8,128)}, f32[2,2,256,256]{3,2,1,0:T(8,128)}, u32[]{:S(2)}, u32[]{:S(2)}) collective-permute-start(f32[2,2,256,256]{3,2,1,0:T(8,128)} %get-tuple-element.70.mine), channel_id=1, source_target_pairs={{0,128},{1,129},{2,130},{3,131},{4,132},{5,133},{6,134},{7,135},{8... | collective-permute-start | bytes 3145736 | tf_op jit(solution)/shard_map/ppermute | solution.py:36
  77.8 4.8 %collective-permute-start.13 = (bf16[16,256,128]{2,1,0:T(8,128)(2,1)}, bf16[16,256,128]{2,1,0:T(8,128)(2,1)}, u32[]{:S(2)}, u32[]{:S(2)}) collective-permute-start(bf16[16,256,128]{2,1,0:T(8,128)(2,1)} %get-tuple-element.72.mine), channel_id=1, source_target_pairs={{0,128},{1,129},{2,130},{3,131},{4,132},{5,133},{6,134},{7,135},{8... | collective-permute-start | bytes 3145736 | tf_op jit(solution)/shard_map/ppermute | solution.py:36
  77.8 26.4 %copy-start.4 = (bf16[16,256,128]{2,1,0:T(8,128)(2,1)S(1)}, bf16[16,256,128]{2,1,0:T(8,128)(2,1)}, u32[]{:S(2)}) copy-start(bf16[16,256,128]{2,1,0:T(8,128)(2,1)} %copy-done.3) | copy-start | bytes 3145732
  108.5 19.5 %all-to-all-start.4 = ((bf16[16,288,128]{2,1,0:T(8,128)(2,1)}), bf16[16,288,128]{2,1,0:T(8,128)(2,1)S(1)}, u32[]{:S(2)}, u32[]{:S(2)}) async-start(bf16[16,288,128]{2,1,0:T(8,128)(2,1)} %copy-done.9), calls=%async_computation.4 | async-start | bytes 2359296 | tf_op jit(solution)/shard_map/all_to_all | solution.py:592
  128.9 11.9 %all-to-all-start.5 = ((f32[8,48,128]{2,1,0:T(8,128)}), f32[8,48,128]{2,1,0:T(8,128)S(1)}, u32[]{:S(2)}, u32[]{:S(2)}) async-start(f32[8,48,128]{2,1,0:T(8,128)} %shard_map.113), calls=%async_computation.5 | async-start | bytes 393216 | tf_op jit(solution)/shard_map/all_to_all | solution.py:595
  140.8 5.8 %collective-permute-start.14 = (f32[80,128]{1,0:T(8,128)S(1)}, f32[80,128]{1,0:T(8,128)S(1)}, u32[]{:S(2)}, u32[]{:S(2)}) collective-permute-start(f32[80,128]{1,0:T(8,128)S(1)} %shard_map.114.mine), channel_id=1, source_target_pairs={{0,128},{1,129},{2,130},{3,131},{4,132},{5,133},{6,134},{7,135},{8... | collective-permute-start | bytes 122888 | tf_op jit(solution)/shard_map/ppermute | solution.py:36
  (7 other events, 15.4 us)

commit v3 on v2

--- a/solution.py
+++ b/solution.py
@@ -551,9 +551,13 @@
     slab, w_oth, s_oth, w_own, s_own, gain_t, gain_s = lax.optimization_barrier(
         (slab, w_oth, s_oth, w_own, s_own, gain_t, gain_s)
     )
-    by_shift = [shift_first(slab, d) for d in (1, 2, 3)]
     (half,) = small_call(squares_kernel, [(8, TOKENS)], slab)
-    (copies,) = small_call(both_kernel, [(NTP, 8, TOKENS)], half, swap_cores(half))
+    slab, half = lax.optimization_barrier((slab, half))
+    half_oth = swap_cores(half)
+    opposite = shift_first(slab, 2)
+    slab, half_oth = lax.optimization_barrier((slab, half_oth))
+    by_shift = [shift_first(slab, 1), opposite, shift_first(slab, 3)]
+    (copies,) = small_call(both_kernel, [(NTP, 8, TOKENS)], half, half_oth)
     widths = (teacher_gain.shape[0], student_gain.shape[0])
     r_t, r_s = small_call(
         functools.partial(scales_kernel, widths),

time: 149 us -> 148 us (level)
  transfers between devices with their start and end apart: 18 -> 18, of which waited for: 9 -> 8; matrix products, arithmetic and copies ran while one was open for 3% -> 3% of each run, Pallas kernels for 12% -> 12%
where the time goes in v3:
time: 148 us; the launch traced here: 147 us
  starting transfers between devices  38.4 us (26%)
  blocking collectives  34.1 us (23%)
  waiting for transfers between devices  31.4 us (21%)
  Pallas kernels  27.4 us (19%)
  local copies, waits for them, and re-layouts  14.2 us (10%)
    ppermute x15, starting transfers between devices, permute(): return lax.ppermute(value, AXES, pairs)  24.8 us
    pallas_call x3, Pallas kernels, partial_logits(): pl.pallas_call(functools.partial(logits_kernel, offsets, first), in_specs...  14.1 us
    all_to_all x1, blocking collectives, on_device(): lax.all_to_all(copies, 'tp', 0, 0, tiled=True)  12.6 us
    all_to_all x1, blocking collectives, on_device(): records = lax.all_to_all(records, 'tp', 0, 0, tiled=True)  11.8 us
    unnamed x26, local copies, waits for them, and re-layouts  11.2 us
    all_to_all x1, waiting for transfers between devices, on_device(): arrived = lax.all_to_all(parts, 'tp', 0, 0, tiled=True)  10.9 us
    all_to_all x1, blocking collectives, on_device(): lax.all_to_all(merge_records(records, NZ), 'tok', 0, 0, tiled=True)  9.71 us
    ppermute x15, waiting for transfers between devices, permute(): return lax.ppermute(value, AXES, pairs)  8.31 us
  transfers between devices with their start and end apart: 18, of which 8 were waited for; matrix products, arithmetic and copies ran while one was open for 3% of the time, Pallas kernels for 12%

profile of v3, /device:TPU:1, one launch (start us, length us, event | category | flops | bytes accessed | tf_op | source)
XLA Modules:
  0.0 147.1 jit_solution(15357653521667790596)
XLA Ops:
  0.6 3.3 %collective-permute-start = (bf16[16,2,512,256]{3,2,1,0:T(8,128)(2,1)}, bf16[16,2,512,256]{3,2,1,0:T(8,128)(2,1)}, u32[]{:S(2)}, u32[]{:S(2)}) collective-permute-start(bf16[16,2,512,256]{3,2,1,0:T(8,128)(2,1)} %bitcast.22), channel_id=1, source_target_pairs={{0,128},{1,129},{2,130},{3,131},{4,132},{5,133},{6,134},{7,135},{8... | collective-permute-start | bytes 25165832 | tf_op jit(solution)/shard_map/ppermute | solution.py:36
  5.5 6.5 %all-to-all-start = ((bf16[8,32,640]{2,1,0:T(8,128)(2,1)}), bf16[8,32,640]{2,1,0:T(8,128)(2,1)S(1)}, u32[]{:S(2)}, u32[]{:S(2)}) async-start(bf16[8,32,640]{2,1,0:T(8,128)(2,1)} %broadcast_in_dim.4), calls=%async_computation | async-start | bytes 655360 | tf_op jit(solution)/shard_map/all_to_all | solution.py:546
  12.0 3.4 %copy-done.5 = bf16[16384,256]{1,0:T(8,128)(2,1)S(1)} copy-done((bf16[16384,256]{1,0:T(8,128)(2,1)S(1)}, bf16[16384,256]{1,0:T(8,128)(2,1)}, u32[]{:S(2)}) %copy-start.5) | copy-done | bytes 8388632
  20.8 4.4 %all-to-all-done = bf16[8,32,640]{2,1,0:T(8,128)(2,1)S(1)} async-done(((bf16[8,32,640]{2,1,0:T(8,128)(2,1)}), bf16[8,32,640]{2,1,0:T(8,128)(2,1)S(1)}, u32[]{:S(2)}, u32[]{:S(2)}) %all-to-all-start) | async-done | bytes 327712 | tf_op jit(solution)/shard_map/all_to_all | solution.py:546
  26.5 2.7 %collective-permute-start.4 = (bf16[256,640]{1,0:T(8,128)(2,1)S(1)}, bf16[256,640]{1,0:T(8,128)(2,1)S(1)}, u32[]{:S(2)}, u32[]{:S(2)}) collective-permute-start(bf16[256,640]{1,0:T(8,128)(2,1)S(1)} %bitcast.25), channel_id=1, source_target_pairs={{0,16},{1,17},{2,18},{3,19},{4,20},{5,21},{6,22},{7,23},{8,24},{9,... | collective-permute-start | bytes 983048 | tf_op jit(solution)/shard_map/ppermute | solution.py:36
  30.7 12.6 %all_to_all.30.squares = f32[16,8,256]{2,1,0:T(8,128)S(1)} all-to-all(f32[16,8,256]{2,1,0:T(8,128)S(1)} %shard_map.104), channel_id=1, replica_groups=mesh['grp'=2,'tp'=16,'tok'=8] {'tp'}, dimensions={0} | all-to-all | bytes 262144 | tf_op jit(solution)/shard_map/all_to_all | solution.py:565
  44.1 2.4 %collective-permute-start.7 = (bf16[2,256,640]{2,1,0:T(8,128)(2,1)S(1)}, bf16[2,256,640]{2,1,0:T(8,128)(2,1)S(1)}, u32[]{:S(2)}, u32[]{:S(2)}) collective-permute-start(bf16[2,256,640]{2,1,0:T(8,128)(2,1)S(1)} %pad_maximum_fusion.1.refs_1_), channel_id=1, source_target_pairs={{0,96},{1,97},{2,98},{3,99},{4,100},{5,101},{6,102},{7,103},{8,104... | collective-permute-start | bytes 1966088 | tf_op jit(solution)/shard_map/ppermute | solution.py:36
  46.5 2.7 %collective-permute-start.11 = (bf16[2,256,640]{2,1,0:T(8,128)(2,1)S(1)}, bf16[2,256,640]{2,1,0:T(8,128)(2,1)S(1)}, u32[]{:S(2)}, u32[]{:S(2)}) collective-permute-start(bf16[2,256,640]{2,1,0:T(8,128)(2,1)S(1)} %pad_maximum_fusion.refs_0_), channel_id=1, source_target_pairs={{0,96},{1,97},{2,98},{3,99},{4,100},{5,101},{6,102},{7,103},{8,104... | collective-permute-start | bytes 1966088 | tf_op jit(solution)/shard_map/ppermute | solution.py:36
  51.4 3.3 %shard_map.106 = (f32[2,2,256,256]{3,2,1,0:T(8,128)S(1)}, bf16[16,256,128]{2,1,0:T(8,128)(2,1)}, bf16[16,256,128]{2,1,0:T(8,128)(2,1)S(1)}) custom-call(bf16[2,256,640]{2,1,0:T(8,128)(2,1)S(1)} %pad_maximum_fusion.refs_0_, bf16[2,256,640]{2,1,0:T(8,128)(2,1)S(1)} %pad_maximum_fusion.1.refs_1_, f32[256,1]{1,0:T(8,128)S(1)} %get-tuple-element.59.refs_2_.refs_4_, ...), custom_call_target="tpu_custom_call" | custom-call | flops 671088640 | bytes 4800000 | tf_op jit(solution)/shard_map/pallas_call | solution.py:173
  54.8 2.7 %collective-permute-start.9 = (bf16[2,256,640]{2,1,0:T(8,128)(2,1)S(1)}, bf16[2,256,640]{2,1,0:T(8,128)(2,1)S(1)}, u32[]{:S(2)}, u32[]{:S(2)}) collective-permute-start(bf16[2,256,640]{2,1,0:T(8,128)(2,1)S(1)} %collective-permute-done.7.refs_3_), channel_id=1, source_target_pairs={{0,96},{1,97},{2,98},{3,99},{4,100},{5,101},{6,102},{7,103},{8,104... | collective-permute-start | bytes 1966088 | tf_op jit(solution)/shard_map/ppermute | solution.py:36
  57.5 4.3 %collective-permute-done.10.refs_1_ = bf16[2,256,640]{2,1,0:T(8,128)(2,1)S(1)} collective-permute-done((bf16[2,256,640]{2,1,0:T(8,128)(2,1)S(1)}, bf16[2,256,640]{2,1,0:T(8,128)(2,1)S(1)}, u32[]{:S(2)}, u32[]{:S(2)}) %collective-permute-start.10) | collective-permute-done | bytes 655392 | tf_op jit(solution)/shard_map/ppermute | solution.py:36
  61.8 6.6 %shard_map.107 = (f32[2,2,256,256]{3,2,1,0:T(8,128)S(1)}, bf16[16,256,128]{2,1,0:T(8,128)(2,1)}, bf16[16,256,128]{2,1,0:T(8,128)(2,1)S(1)}) custom-call(bf16[2,256,640]{2,1,0:T(8,128)(2,1)S(1)} %collective-permute-done.6.refs_0_, bf16[2,256,640]{2,1,0:T(8,128)(2,1)S(1)} %collective-permute-done.10.refs_1_, ...), custom_call_target="tpu_custom_call", output_to_operand_aliasing={{1}: (13, {}), {2}: (14, {})} | custom-call | flops 1342177280 | bytes 9600000 | tf_op jit(solution)/shard_map/pallas_call | solution.py:173
  68.8 4.2 %shard_map.108 = (f32[2,2,256,256]{3,2,1,0:T(8,128)}, bf16[16,256,128]{2,1,0:T(8,128)(2,1)}, bf16[16,256,128]{2,1,0:T(8,128)(2,1)S(1)}) custom-call(bf16[2,256,640]{2,1,0:T(8,128)(2,1)S(1)} %collective-permute-done.8.refs_0_, bf16[2,256,640]{2,1,0:T(8,128)(2,1)S(1)} %collective-permute-done.9.refs_1_, ...), custom_call_target="tpu_custom_call", output_to_operand_aliasing={{1}: (11, {}), {2}: (12, {})} | custom-call | flops 671088640 | bytes 4800000 | tf_op jit(solution)/shard_map/pallas_call | solution.py:173
  74.1 3.1 %collective-permute-start.12 = (f32[2,2,256,256]{3,2,1,0:T(8,128)}, f32[2,2,256,256]{3,2,1,0:T(8,128)}, u32[]{:S(2)}, u32[]{:S(2)}) collective-permute-start(f32[2,2,256,256]{3,2,1,0:T(8,128)} %get-tuple-element.78.mine), channel_id=1, source_target_pairs={{0,128},{1,129},{2,130},{3,131},{4,132},{5,133},{6,134},{7,135},{8... | collective-permute-start | bytes 3145736 | tf_op jit(solution)/shard_map/ppermute | solution.py:36
  77.3 2.5 %collective-permute-done.12.other = f32[2,2,256,256]{3,2,1,0:T(8,128)} collective-permute-done((f32[2,2,256,256]{3,2,1,0:T(8,128)}, f32[2,2,256,256]{3,2,1,0:T(8,128)}, u32[]{:S(2)}, u32[]{:S(2)}) %collective-permute-start.12) | collective-permute-done | bytes 1048608 | tf_op jit(solution)/shard_map/ppermute | solution.py:36
  82.0 11.8 %all_to_all.31.records = f32[16,8,256]{2,1,0:T(8,128)S(1)} all-to-all(f32[16,8,256]{2,1,0:T(8,128)S(1)} %get-tuple-element.81), channel_id=1, replica_groups=mesh['grp'=2,'tp'=16,'tok'=8] {'tp'}, dimensions={0} | all-to-all | bytes 262144 | tf_op jit(solution)/shard_map/all_to_all | solution.py:591
  93.9 9.7 %all_to_all.32.records = f32[8,8,256]{2,1,0:T(8,128)S(1)} all-to-all(f32[8,8,256]{2,1,0:T(8,128)S(1)} %shard_map.110), channel_id=1, replica_groups=mesh['grp'=2,'tp'=16,'tok'=8] {'tok'}, dimensions={0} | all-to-all | bytes 131072 | tf_op jit(solution)/shard_map/all_to_all | solution.py:592
  103.6 3.4 %shard_map.111 = (bf16[16,288,128]{2,1,0:T(8,128)(2,1)S(1)}, bf16[256,256]{1,0:T(8,128)(2,1)S(1)}, f32[1,256]{1,0:T(1,128)}) custom-call(s32[3]{0:T(128)S(1)} %pad_add_fusion.base, f32[8,8,256]{2,1,0:T(8,128)S(1)} %all_to_all.32.records, f32[2,256,512]{2,1,0:T(8,128)S(1)} %get-tuple-element.82.both, s32[1,256]{1,0:T(1,128)S(1)} %bitcast.38, ...), custom_call_target="tpu_custom_call" | custom-call | tf_op jit(solution)/shard_map/pallas_call | solution.py:359
  108.0 3.7 %all-to-all-start.4 = ((bf16[16,288,128]{2,1,0:T(8,128)(2,1)}), bf16[16,288,128]{2,1,0:T(8,128)(2,1)S(1)}, u32[]{:S(2)}, u32[]{:S(2)}) async-start(bf16[16,288,128]{2,1,0:T(8,128)(2,1)} %copy-done.9), calls=%async_computation.4 | async-start | bytes 2359296 | tf_op jit(solution)/shard_map/all_to_all | solution.py:596
  111.7 4.9 %shard_map.112 = bf16[16,2,128,256]{3,2,1,0:T(8,128)(2,1)} custom-call(s32[3]{0:T(128)S(1)} %pad_add_fusion.base, bf16[16,256,128]{2,1,0:T(8,128)(2,1)} %get-tuple-element.80.mine, bf16[16,256,128]{2,1,0:T(8,128)(2,1)} %collective-permute-done.13.other, bf16[256,256]{1,0:T(8,128)(2,1)S(1)} %get-tuple-element.87.grad), custom_call_target="tpu_custom_call" | custom-call | flops 536870912 | bytes 4500000 | tf_op jit(solution)/shard_map/pallas_call | solution.py:387
  116.6 10.9 %all-to-all-done.4.parts = bf16[16,288,128]{2,1,0:T(8,128)(2,1)S(1)} async-done(((bf16[16,288,128]{2,1,0:T(8,128)(2,1)}), bf16[16,288,128]{2,1,0:T(8,128)(2,1)S(1)}, u32[]{:S(2)}, u32[]{:S(2)}) %all-to-all-start.4) | async-done | bytes 1179680 | tf_op jit(solution)/shard_map/all_to_all | solution.py:596
  128.3 3.4 %all-to-all-start.5 = ((f32[8,48,128]{2,1,0:T(8,128)}), f32[8,48,128]{2,1,0:T(8,128)S(1)}, u32[]{:S(2)}, u32[]{:S(2)}) async-start(f32[8,48,128]{2,1,0:T(8,128)} %shard_map.113), calls=%async_computation.5 | async-start | bytes 393216 | tf_op jit(solution)/shard_map/all_to_all | solution.py:599
  132.5 7.8 %all-to-all-done.5.parts = f32[8,48,128]{2,1,0:T(8,128)S(1)} async-done(((f32[8,48,128]{2,1,0:T(8,128)}), f32[8,48,128]{2,1,0:T(8,128)S(1)}, u32[]{:S(2)}, u32[]{:S(2)}) %all-to-all-start.5) | async-done | bytes 196640 | tf_op jit(solution)/shard_map/all_to_all | solution.py:599
  140.3 4.9 %collective-permute-start.14 = (f32[80,128]{1,0:T(8,128)S(1)}, f32[80,128]{1,0:T(8,128)S(1)}, u32[]{:S(2)}, u32[]{:S(2)}) collective-permute-start(f32[80,128]{1,0:T(8,128)S(1)} %shard_map.114.mine), channel_id=1, source_target_pairs={{0,128},{1,129},{2,130},{3,131},{4,132},{5,133},{6,134},{7,135},{8... | collective-permute-start | bytes 122888 | tf_op jit(solution)/shard_map/ppermute | solution.py:36
  (66 shorter events, 21.1 us)
Async XLA Ops:
  0.6 24.6 %collective-permute-start = (bf16[16,2,512,256]{3,2,1,0:T(8,128)(2,1)}, bf16[16,2,512,256]{3,2,1,0:T(8,128)(2,1)}, u32[]{:S(2)}, u32[]{:S(2)}) collective-permute-start(bf16[16,2,512,256]{3,2,1,0:T(8,128)(2,1)} %bitcast.22), channel_id=1, source_target_pairs={{0,128},{1,129},{2,130},{3,131},{4,132},{5,133},{6,134},{7,135},{8... | collective-permute-start | bytes 25165832 | tf_op jit(solution)/shard_map/ppermute | solution.py:36
  4.0 21.3 %collective-permute-start.1 = (bf16[16,2,128,256]{3,2,1,0:T(8,128)(2,1)}, bf16[16,2,128,256]{3,2,1,0:T(8,128)(2,1)S(1)}, u32[]{:S(2)}, u32[]{:S(2)}) collective-permute-start(bf16[16,2,128,256]{3,2,1,0:T(8,128)(2,1)} %bitcast.29), channel_id=1, source_target_pairs={{0,128},{1,129},{2,130},{3,131},{4,132},{5,133},{6,134},{7,135},{8... | collective-permute-start | bytes 6291464 | tf_op jit(solution)/shard_map/ppermute | solution.py:36
  5.5 19.7 %all-to-all-start = ((bf16[8,32,640]{2,1,0:T(8,128)(2,1)}), bf16[8,32,640]{2,1,0:T(8,128)(2,1)S(1)}, u32[]{:S(2)}, u32[]{:S(2)}) async-start(bf16[8,32,640]{2,1,0:T(8,128)(2,1)} %broadcast_in_dim.4), calls=%async_computation | async-start | bytes 655360 | tf_op jit(solution)/shard_map/all_to_all | solution.py:546
  19.4 29.8 %copy-start.11 = (f32[4096]{0:T(1024)S(1)}, f32[4096]{0:T(1024)}, u32[]{:S(2)}) copy-start(f32[4096]{0:T(1024)} %param.11) | copy-start | bytes 49156
  25.3 23.9 %copy-start.10 = (f32[32,512]{1,0:T(8,128)S(1)}, f32[32,512]{1,0:T(8,128)}, u32[]{:S(2)}) copy-start(f32[32,512]{1,0:T(8,128)} %reshape.44.refs_4_.refs_6_) | copy-start | bytes 196612
  25.5 3.8 %collective-permute-start.2 = (f32[8,256]{1,0:T(8,128)S(1)}, f32[8,256]{1,0:T(8,128)S(1)}, u32[]{:S(2)}, u32[]{:S(2)}) collective-permute-start(f32[8,256]{1,0:T(8,128)S(1)} %shard_map.103.mine), channel_id=1, source_target_pairs={{0,128},{1,129},{2,130},{3,131},{4,132},{5,133},{6,134},{7,135},{8... | collective-permute-start | bytes 24584 | tf_op jit(solution)/shard_map/ppermute | solution.py:36
  26.5 17.1 %collective-permute-start.4 = (bf16[256,640]{1,0:T(8,128)(2,1)S(1)}, bf16[256,640]{1,0:T(8,128)(2,1)S(1)}, u32[]{:S(2)}, u32[]{:S(2)}) collective-permute-start(bf16[256,640]{1,0:T(8,128)(2,1)S(1)} %bitcast.25), channel_id=1, source_target_pairs={{0,16},{1,17},{2,18},{3,19},{4,20},{5,21},{6,22},{7,23},{8,24},{9,... | collective-permute-start | bytes 983048 | tf_op jit(solution)/shard_map/ppermute | solution.py:36
  29.2 14.3 %collective-permute-start.5 = (bf16[256,640]{1,0:T(8,128)(2,1)S(1)}, bf16[256,640]{1,0:T(8,128)(2,1)S(1)}, u32[]{:S(2)}, u32[]{:S(2)}) collective-permute-start(bf16[256,640]{1,0:T(8,128)(2,1)S(1)} %bitcast.26), channel_id=1, source_target_pairs={{0,24},{1,25},{2,26},{3,27},{4,28},{5,29},{6,30},{7,31},{8,0},{9,1... | collective-permute-start | bytes 983048 | tf_op jit(solution)/shard_map/ppermute | solution.py:36
  30.1 13.6 %collective-permute-start.3 = (bf16[256,640]{1,0:T(8,128)(2,1)S(1)}, bf16[256,640]{1,0:T(8,128)(2,1)S(1)}, u32[]{:S(2)}, u32[]{:S(2)}) collective-permute-start(bf16[256,640]{1,0:T(8,128)(2,1)S(1)} %bitcast.27), channel_id=1, source_target_pairs={{0,8},{1,9},{2,10},{3,11},{4,12},{5,13},{6,14},{7,15},{8,16},{9,17... | collective-permute-start | bytes 983048 | tf_op jit(solution)/shard_map/ppermute | solution.py:36
  43.5 25.3 %copy-start.6 = (f32[256,1]{1,0:T(8,128)}, f32[256,1]{1,0:T(8,128)S(1)}, u32[]{:S(2)}) copy-start(f32[256,1]{1,0:T(8,128)S(1)} %get-tuple-element.60.refs_3_.refs_5_.r_s) | copy-start | bytes 3076
  43.7 11.0 %collective-permute-start.6 = (bf16[2,256,640]{2,1,0:T(8,128)(2,1)S(1)}, bf16[2,256,640]{2,1,0:T(8,128)(2,1)S(1)}, u32[]{:S(2)}, u32[]{:S(2)}) collective-permute-start(bf16[2,256,640]{2,1,0:T(8,128)(2,1)S(1)} %pad_maximum_fusion.refs_0_), channel_id=1, source_target_pairs={{0,32},{1,33},{2,34},{3,35},{4,36},{5,37},{6,38},{7,39},{8,40},{9,... | collective-permute-start | bytes 1966088 | tf_op jit(solution)/shard_map/ppermute | solution.py:36
  44.1 10.7 %collective-permute-start.7 = (bf16[2,256,640]{2,1,0:T(8,128)(2,1)S(1)}, bf16[2,256,640]{2,1,0:T(8,128)(2,1)S(1)}, u32[]{:S(2)}, u32[]{:S(2)}) collective-permute-start(bf16[2,256,640]{2,1,0:T(8,128)(2,1)S(1)} %pad_maximum_fusion.1.refs_1_), channel_id=1, source_target_pairs={{0,96},{1,97},{2,98},{3,99},{4,100},{5,101},{6,102},{7,103},{8,104... | collective-permute-start | bytes 1966088 | tf_op jit(solution)/shard_map/ppermute | solution.py:36
  46.5 15.3 %collective-permute-start.10 = (bf16[2,256,640]{2,1,0:T(8,128)(2,1)S(1)}, bf16[2,256,640]{2,1,0:T(8,128)(2,1)S(1)}, u32[]{:S(2)}, u32[]{:S(2)}) collective-permute-start(bf16[2,256,640]{2,1,0:T(8,128)(2,1)S(1)} %pad_maximum_fusion.1.refs_1_), channel_id=1, source_target_pairs={{0,32},{1,33},{2,34},{3,35},{4,36},{5,37},{6,38},{7,39},{8,40},{9,... | collective-permute-start | bytes 1966088 | tf_op jit(solution)/shard_map/ppermute | solution.py:36
  46.5 15.3 %collective-permute-start.11 = (bf16[2,256,640]{2,1,0:T(8,128)(2,1)S(1)}, bf16[2,256,640]{2,1,0:T(8,128)(2,1)S(1)}, u32[]{:S(2)}, u32[]{:S(2)}) collective-permute-start(bf16[2,256,640]{2,1,0:T(8,128)(2,1)S(1)} %pad_maximum_fusion.refs_0_), channel_id=1, source_target_pairs={{0,96},{1,97},{2,98},{3,99},{4,100},{5,101},{6,102},{7,103},{8,104... | collective-permute-start | bytes 1966088 | tf_op jit(solution)/shard_map/ppermute | solution.py:36
  54.8 14.0 %collective-permute-start.8 = (bf16[2,256,640]{2,1,0:T(8,128)(2,1)S(1)}, bf16[2,256,640]{2,1,0:T(8,128)(2,1)S(1)}, u32[]{:S(2)}, u32[]{:S(2)}) collective-permute-start(bf16[2,256,640]{2,1,0:T(8,128)(2,1)S(1)} %collective-permute-done.6.refs_0_), channel_id=1, source_target_pairs={{0,32},{1,33},{2,34},{3,35},{4,36},{5,37},{6,38},{7,39},{8,40},{9,... | collective-permute-start | bytes 1966088 | tf_op jit(solution)/shard_map/ppermute | solution.py:36
  54.8 14.0 %collective-permute-start.9 = (bf16[2,256,640]{2,1,0:T(8,128)(2,1)S(1)}, bf16[2,256,640]{2,1,0:T(8,128)(2,1)S(1)}, u32[]{:S(2)}, u32[]{:S(2)}) collective-permute-start(bf16[2,256,640]{2,1,0:T(8,128)(2,1)S(1)} %collective-permute-done.7.refs_3_), channel_id=1, source_target_pairs={{0,96},{1,97},{2,98},{3,99},{4,100},{5,101},{6,102},{7,103},{8,104... | collective-permute-start | bytes 1966088 | tf_op jit(solution)/shard_map/ppermute | solution.py:36
  68.8 11.0 %copy-start.12 = (s32[256]{0:T(256)S(1)}, s32[256]{0:T(256)}, u32[]{:S(2)}) copy-start(s32[256]{0:T(256)} %param.13) | copy-start | bytes 3076
  74.1 29.5 %copy-start.7 = (f32[256,1]{1,0:T(8,128)S(1)}, f32[256,1]{1,0:T(8,128)}, u32[]{:S(2)}) copy-start(f32[256,1]{1,0:T(8,128)} %copy-done.6) | copy-start | bytes 3076
  74.1 5.8 %collective-permute-start.12 = (f32[2,2,256,256]{3,2,1,0:T(8,128)}, f32[2,2,256,256]{3,2,1,0:T(8,128)}, u32[]{:S(2)}, u32[]{:S(2)}) collective-permute-start(f32[2,2,256,256]{3,2,1,0:T(8,128)} %get-tuple-element.78.mine), channel_id=1, source_target_pairs={{0,128},{1,129},{2,130},{3,131},{4,132},{5,133},{6,134},{7,135},{8... | collective-permute-start | bytes 3145736 | tf_op jit(solution)/shard_map/ppermute | solution.py:36
  77.2 4.8 %collective-permute-start.13 = (bf16[16,256,128]{2,1,0:T(8,128)(2,1)}, bf16[16,256,128]{2,1,0:T(8,128)(2,1)}, u32[]{:S(2)}, u32[]{:S(2)}) collective-permute-start(bf16[16,256,128]{2,1,0:T(8,128)(2,1)} %get-tuple-element.80.mine), channel_id=1, source_target_pairs={{0,128},{1,129},{2,130},{3,131},{4,132},{5,133},{6,134},{7,135},{8... | collective-permute-start | bytes 3145736 | tf_op jit(solution)/shard_map/ppermute | solution.py:36
  77.2 26.4 %copy-start.4 = (bf16[16,256,128]{2,1,0:T(8,128)(2,1)S(1)}, bf16[16,256,128]{2,1,0:T(8,128)(2,1)}, u32[]{:S(2)}) copy-start(bf16[16,256,128]{2,1,0:T(8,128)(2,1)} %copy-done.3) | copy-start | bytes 3145732
  108.0 19.5 %all-to-all-start.4 = ((bf16[16,288,128]{2,1,0:T(8,128)(2,1)}), bf16[16,288,128]{2,1,0:T(8,128)(2,1)S(1)}, u32[]{:S(2)}, u32[]{:S(2)}) async-start(bf16[16,288,128]{2,1,0:T(8,128)(2,1)} %copy-done.9), calls=%async_computation.4 | async-start | bytes 2359296 | tf_op jit(solution)/shard_map/all_to_all | solution.py:596
  128.3 11.9 %all-to-all-start.5 = ((f32[8,48,128]{2,1,0:T(8,128)}), f32[8,48,128]{2,1,0:T(8,128)S(1)}, u32[]{:S(2)}, u32[]{:S(2)}) async-start(f32[8,48,128]{2,1,0:T(8,128)} %shard_map.113), calls=%async_computation.5 | async-start | bytes 393216 | tf_op jit(solution)/shard_map/all_to_all | solution.py:599
  140.3 5.8 %collective-permute-start.14 = (f32[80,128]{1,0:T(8,128)S(1)}, f32[80,128]{1,0:T(8,128)S(1)}, u32[]{:S(2)}, u32[]{:S(2)}) collective-permute-start(f32[80,128]{1,0:T(8,128)S(1)} %shard_map.114.mine), channel_id=1, source_target_pairs={{0,128},{1,129},{2,130},{3,131},{4,132},{5,133},{6,134},{7,135},{8... | collective-permute-start | bytes 122888 | tf_op jit(solution)/shard_map/ppermute | solution.py:36
  (7 other events, 15.4 us)

commit v4 on v3

--- a/solution.py
+++ b/solution.py
@@ -587,7 +587,9 @@
     targets_row = targets[None, :]
     both, records = local_stats(base, half, swap_cores(half), targets_row)
     normed_oth = swap_cores(normed_s)
-    records, normed_oth = lax.optimization_barrier((records, normed_oth))
+    hidden_rows = lax.dynamic_slice_in_dim(raw_s, tp * 16 + z * 2, 2, 1)
+    hidden_rows = hidden_rows.astype(F32).transpose(1, 0, 2).reshape(32, KS)
+    records, normed_oth, hidden_rows = lax.optimization_barrier((records, normed_oth, hidden_rows))
     records = lax.all_to_all(records, "tp", 0, 0, tiled=True)
     records = lax.all_to_all(merge_records(records, NZ), "tok", 0, 0, tiled=True)
     parts, grad_own, loss = grad_parts(
@@ -597,8 +599,6 @@
     d_head = head_gradient(base, normed_s, normed_oth, grad_own)
     arrived, d_head = lax.optimization_barrier((arrived, d_head))
     arrived = lax.all_to_all(fold_parts(arrived), "tok", 0, 0, tiled=True)
-    hidden_rows = lax.dynamic_slice_in_dim(raw_s, tp * 16 + z * 2, 2, 1)
-    hidden_rows = hidden_rows.astype(F32).transpose(1, 0, 2).reshape(32, KS)
     mine = sum_parts(arrived, hidden_rows)
     hidden_gradient, gain_gradient = norm_backward(
         mine, swap_cores(mine), student_gain.reshape(NTP, 2, KS).transpose(1, 0, 2)

time: 148 us -> 148 us (level)
  blocking collectives: 34.1 us -> 45.1 us
  waiting for transfers between devices: 31.4 us -> 22.8 us
  starting transfers between devices: 38.4 us -> 35.6 us
    all_to_all x0 -> x1, blocking collectives: none -> 11 us  [on_device(): arrived = lax.all_to_all(fold_parts(arrived), 'tok', 0, 0, tiled=True)]
    all_to_all x1 -> x0, waiting for transfers between devices: 7.76 us -> none  [on_device(): arrived = lax.all_to_all(fold_parts(arrived), 'tok', 0, 0, tiled=True)]
    all_to_all x1 -> x0, starting transfers between devices: 3.39 us -> none  [on_device(): arrived = lax.all_to_all(fold_parts(arrived), 'tok', 0, 0, tiled=True)]
  transfers between devices with their start and end apart: 18 -> 17, of which waited for: 8 -> 7; matrix products, arithmetic and copies ran while one was open for 3% -> 3% of each run, Pallas kernels for 12% -> 12%
where the time goes in v4:
time: 148 us
  blocking collectives  45.1 us (30%)
  starting transfers between devices  35.6 us (24%)
  Pallas kernels  28 us (19%)
  waiting for transfers between devices  22.8 us (15%)
  local copies, waits for them, and re-layouts  14.1 us (10%)
    ppermute x15, starting transfers between devices, permute(): return lax.ppermute(value, AXES, pairs)  24.8 us
    pallas_call x3, Pallas kernels, partial_logits(): pl.pallas_call(functools.partial(logits_kernel, offsets, first), in_specs...  14.1 us
    all_to_all x1, blocking collectives, on_device(): lax.all_to_all(copies, 'tp', 0, 0, tiled=True)  12.6 us
    all_to_all x1, blocking collectives, on_device(): records = lax.all_to_all(records, 'tp', 0, 0, tiled=True)  11.8 us
    unnamed x26, local copies, waits for them, and re-layouts  11.2 us
    all_to_all x1, blocking collectives, on_device(): arrived = lax.all_to_all(fold_parts(arrived), 'tok', 0, 0, tiled=True)  11 us
    all_to_all x1, waiting for transfers between devices, on_device(): arrived = lax.all_to_all(parts, 'tp', 0, 0, tiled=True)  10.9 us
    all_to_all x1, blocking collectives, on_device(): lax.all_to_all(merge_records(records, NZ), 'tok', 0, 0, tiled=True)  9.71 us
  transfers between devices with their start and end apart: 17, of which 7 were waited for; matrix products, arithmetic and copies ran while one was open for 3% of the time, Pallas kernels for 12%

profile of v4, /device:TPU:1, one launch (start us, length us, event | category | flops | bytes accessed | tf_op | source)
XLA Modules:
  0.0 147.5 jit_solution(14661936801985092281)
XLA Ops:
  0.6 3.3 %collective-permute-start = (bf16[16,2,512,256]{3,2,1,0:T(8,128)(2,1)}, bf16[16,2,512,256]{3,2,1,0:T(8,128)(2,1)}, u32[]{:S(2)}, u32[]{:S(2)}) collective-permute-start(bf16[16,2,512,256]{3,2,1,0:T(8,128)(2,1)} %bitcast.22), channel_id=1, source_target_pairs={{0,128},{1,129},{2,130},{3,131},{4,132},{5,133},{6,134},{7,135},{8... | collective-permute-start | bytes 25165832 | tf_op jit(solution)/shard_map/ppermute | solution.py:36
  5.5 6.5 %all-to-all-start = ((bf16[8,32,640]{2,1,0:T(8,128)(2,1)}), bf16[8,32,640]{2,1,0:T(8,128)(2,1)S(1)}, u32[]{:S(2)}, u32[]{:S(2)}) async-start(bf16[8,32,640]{2,1,0:T(8,128)(2,1)} %broadcast_in_dim.4), calls=%async_computation | async-start | bytes 655360 | tf_op jit(solution)/shard_map/all_to_all | solution.py:546
  12.0 3.4 %copy-done.5 = bf16[16384,256]{1,0:T(8,128)(2,1)S(1)} copy-done((bf16[16384,256]{1,0:T(8,128)(2,1)S(1)}, bf16[16384,256]{1,0:T(8,128)(2,1)}, u32[]{:S(2)}) %copy-start.5) | copy-done | bytes 8388632
  20.8 4.5 %all-to-all-done = bf16[8,32,640]{2,1,0:T(8,128)(2,1)S(1)} async-done(((bf16[8,32,640]{2,1,0:T(8,128)(2,1)}), bf16[8,32,640]{2,1,0:T(8,128)(2,1)S(1)}, u32[]{:S(2)}, u32[]{:S(2)}) %all-to-all-start) | async-done | bytes 327712 | tf_op jit(solution)/shard_map/all_to_all | solution.py:546
  26.5 2.7 %collective-permute-start.4 = (bf16[256,640]{1,0:T(8,128)(2,1)S(1)}, bf16[256,640]{1,0:T(8,128)(2,1)S(1)}, u32[]{:S(2)}, u32[]{:S(2)}) collective-permute-start(bf16[256,640]{1,0:T(8,128)(2,1)S(1)} %bitcast.25), channel_id=1, source_target_pairs={{0,16},{1,17},{2,18},{3,19},{4,20},{5,21},{6,22},{7,23},{8,24},{9,... | collective-permute-start | bytes 983048 | tf_op jit(solution)/shard_map/ppermute | solution.py:36
  30.7 12.6 %all_to_all.30.squares = f32[16,8,256]{2,1,0:T(8,128)S(1)} all-to-all(f32[16,8,256]{2,1,0:T(8,128)S(1)} %shard_map.104), channel_id=1, replica_groups=mesh['grp'=2,'tp'=16,'tok'=8] {'tp'}, dimensions={0} | all-to-all | bytes 262144 | tf_op jit(solution)/shard_map/all_to_all | solution.py:565
  44.1 2.4 %collective-permute-start.7 = (bf16[2,256,640]{2,1,0:T(8,128)(2,1)S(1)}, bf16[2,256,640]{2,1,0:T(8,128)(2,1)S(1)}, u32[]{:S(2)}, u32[]{:S(2)}) collective-permute-start(bf16[2,256,640]{2,1,0:T(8,128)(2,1)S(1)} %pad_maximum_fusion.1.refs_1_), channel_id=1, source_target_pairs={{0,96},{1,97},{2,98},{3,99},{4,100},{5,101},{6,102},{7,103},{8,104... | collective-permute-start | bytes 1966088 | tf_op jit(solution)/shard_map/ppermute | solution.py:36
  46.5 2.7 %collective-permute-start.11 = (bf16[2,256,640]{2,1,0:T(8,128)(2,1)S(1)}, bf16[2,256,640]{2,1,0:T(8,128)(2,1)S(1)}, u32[]{:S(2)}, u32[]{:S(2)}) collective-permute-start(bf16[2,256,640]{2,1,0:T(8,128)(2,1)S(1)} %pad_maximum_fusion.refs_0_), channel_id=1, source_target_pairs={{0,96},{1,97},{2,98},{3,99},{4,100},{5,101},{6,102},{7,103},{8,104... | collective-permute-start | bytes 1966088 | tf_op jit(solution)/shard_map/ppermute | solution.py:36
  49.2 2.2 %copy-done.2 = bf16[16,512,256]{2,1,0:T(8,128)(2,1)S(1)} copy-done((bf16[16,512,256]{2,1,0:T(8,128)(2,1)S(1)}, bf16[16,512,256]{2,1,0:T(8,128)(2,1)}, u32[]{:S(2)}) %copy-start.2) | copy-done | bytes 4194328
  51.4 3.3 %shard_map.106 = (f32[2,2,256,256]{3,2,1,0:T(8,128)S(1)}, bf16[16,256,128]{2,1,0:T(8,128)(2,1)}, bf16[16,256,128]{2,1,0:T(8,128)(2,1)S(1)}) custom-call(bf16[2,256,640]{2,1,0:T(8,128)(2,1)S(1)} %pad_maximum_fusion.refs_0_, bf16[2,256,640]{2,1,0:T(8,128)(2,1)S(1)} %pad_maximum_fusion.1.refs_1_, f32[256,1]{1,0:T(8,128)S(1)} %get-tuple-element.60.refs_2_.refs_4_, ...), custom_call_target="tpu_custom_call" | custom-call | flops 671088640 | bytes 4800000 | tf_op jit(solution)/shard_map/pallas_call | solution.py:173
  54.8 2.7 %collective-permute-start.9 = (bf16[2,256,640]{2,1,0:T(8,128)(2,1)S(1)}, bf16[2,256,640]{2,1,0:T(8,128)(2,1)S(1)}, u32[]{:S(2)}, u32[]{:S(2)}) collective-permute-start(bf16[2,256,640]{2,1,0:T(8,128)(2,1)S(1)} %collective-permute-done.7.refs_3_), channel_id=1, source_target_pairs={{0,96},{1,97},{2,98},{3,99},{4,100},{5,101},{6,102},{7,103},{8,104... | collective-permute-start | bytes 1966088 | tf_op jit(solution)/shard_map/ppermute | solution.py:36
  57.5 4.3 %collective-permute-done.10.refs_1_ = bf16[2,256,640]{2,1,0:T(8,128)(2,1)S(1)} collective-permute-done((bf16[2,256,640]{2,1,0:T(8,128)(2,1)S(1)}, bf16[2,256,640]{2,1,0:T(8,128)(2,1)S(1)}, u32[]{:S(2)}, u32[]{:S(2)}) %collective-permute-start.10) | collective-permute-done | bytes 655392 | tf_op jit(solution)/shard_map/ppermute | solution.py:36
  61.8 6.6 %shard_map.107 = (f32[2,2,256,256]{3,2,1,0:T(8,128)S(1)}, bf16[16,256,128]{2,1,0:T(8,128)(2,1)}, bf16[16,256,128]{2,1,0:T(8,128)(2,1)S(1)}) custom-call(bf16[2,256,640]{2,1,0:T(8,128)(2,1)S(1)} %collective-permute-done.6.refs_0_, bf16[2,256,640]{2,1,0:T(8,128)(2,1)S(1)} %collective-permute-done.10.refs_1_, ...), custom_call_target="tpu_custom_call", output_to_operand_aliasing={{1}: (13, {}), {2}: (14, {})} | custom-call | flops 1342177280 | bytes 9600000 | tf_op jit(solution)/shard_map/pallas_call | solution.py:173
  68.8 4.2 %shard_map.108 = (f32[2,2,256,256]{3,2,1,0:T(8,128)}, bf16[16,256,128]{2,1,0:T(8,128)(2,1)}, bf16[16,256,128]{2,1,0:T(8,128)(2,1)S(1)}) custom-call(bf16[2,256,640]{2,1,0:T(8,128)(2,1)S(1)} %collective-permute-done.8.refs_0_, bf16[2,256,640]{2,1,0:T(8,128)(2,1)S(1)} %collective-permute-done.9.refs_1_, ...), custom_call_target="tpu_custom_call", output_to_operand_aliasing={{1}: (11, {}), {2}: (12, {})} | custom-call | flops 671088640 | bytes 4800000 | tf_op jit(solution)/shard_map/pallas_call | solution.py:173
  74.1 3.1 %collective-permute-start.12 = (f32[2,2,256,256]{3,2,1,0:T(8,128)}, f32[2,2,256,256]{3,2,1,0:T(8,128)}, u32[]{:S(2)}, u32[]{:S(2)}) collective-permute-start(f32[2,2,256,256]{3,2,1,0:T(8,128)} %get-tuple-element.79.mine), channel_id=1, source_target_pairs={{0,128},{1,129},{2,130},{3,131},{4,132},{5,133},{6,134},{7,135},{8... | collective-permute-start | bytes 3145736 | tf_op jit(solution)/shard_map/ppermute | solution.py:36
  79.8 2.1 %shard_map.109 = (f32[2,256,512]{2,1,0:T(8,128)S(1)}, f32[16,8,256]{2,1,0:T(8,128)S(1)}) custom-call(s32[3]{0:T(128)S(1)} %pad_add_fusion.base, f32[2,2,256,256]{3,2,1,0:T(8,128)} %get-tuple-element.79.mine, f32[2,2,256,256]{3,2,1,0:T(8,128)} %collective-permute-done.12.other, s32[1,256]{1,0:T(1,128)S(1)} %bitcast.37), custom_call_target="tpu_custom_call" | custom-call | tf_op jit(solution)/shard_map/pallas_call | solution.py:241
  82.0 11.8 %all_to_all.31.records = f32[16,8,256]{2,1,0:T(8,128)S(1)} all-to-all(f32[16,8,256]{2,1,0:T(8,128)S(1)} %get-tuple-element.83), channel_id=1, replica_groups=mesh['grp'=2,'tp'=16,'tok'=8] {'tp'}, dimensions={0} | all-to-all | bytes 262144 | tf_op jit(solution)/shard_map/all_to_all | solution.py:593
  93.8 9.7 %all_to_all.32.records = f32[8,8,256]{2,1,0:T(8,128)S(1)} all-to-all(f32[8,8,256]{2,1,0:T(8,128)S(1)} %shard_map.110), channel_id=1, replica_groups=mesh['grp'=2,'tp'=16,'tok'=8] {'tok'}, dimensions={0} | all-to-all | bytes 131072 | tf_op jit(solution)/shard_map/all_to_all | solution.py:594
  103.6 3.4 %shard_map.111 = (bf16[16,288,128]{2,1,0:T(8,128)(2,1)S(1)}, bf16[256,256]{1,0:T(8,128)(2,1)S(1)}, f32[1,256]{1,0:T(1,128)}) custom-call(s32[3]{0:T(128)S(1)} %pad_add_fusion.base, f32[8,8,256]{2,1,0:T(8,128)S(1)} %all_to_all.32.records, f32[2,256,512]{2,1,0:T(8,128)S(1)} %get-tuple-element.84.both, s32[1,256]{1,0:T(1,128)S(1)} %bitcast.38, ...), custom_call_target="tpu_custom_call" | custom-call | tf_op jit(solution)/shard_map/pallas_call | solution.py:359
  107.9 4.4 %all-to-all-start.4 = ((bf16[16,288,128]{2,1,0:T(8,128)(2,1)}), bf16[16,288,128]{2,1,0:T(8,128)(2,1)}, u32[]{:S(2)}, u32[]{:S(2)}) async-start(bf16[16,288,128]{2,1,0:T(8,128)(2,1)} %copy-done.9), calls=%async_computation.4 | async-start | bytes 2359296 | tf_op jit(solution)/shard_map/all_to_all | solution.py:598
  112.3 4.9 %shard_map.112 = bf16[16,2,128,256]{3,2,1,0:T(8,128)(2,1)} custom-call(s32[3]{0:T(128)S(1)} %pad_add_fusion.base, bf16[16,256,128]{2,1,0:T(8,128)(2,1)} %get-tuple-element.81.mine, bf16[16,256,128]{2,1,0:T(8,128)(2,1)} %collective-permute-done.13.other, bf16[256,256]{1,0:T(8,128)(2,1)S(1)} %get-tuple-element.88.grad), custom_call_target="tpu_custom_call" | custom-call | flops 536870912 | bytes 4500000 | tf_op jit(solution)/shard_map/pallas_call | solution.py:387
  117.2 10.9 %all-to-all-done.4.parts = bf16[16,288,128]{2,1,0:T(8,128)(2,1)} async-done(((bf16[16,288,128]{2,1,0:T(8,128)(2,1)}), bf16[16,288,128]{2,1,0:T(8,128)(2,1)}, u32[]{:S(2)}, u32[]{:S(2)}) %all-to-all-start.4) | async-done | bytes 1179680 | tf_op jit(solution)/shard_map/all_to_all | solution.py:598
  129.6 11.0 %all_to_all.33.parts = f32[8,48,128]{2,1,0:T(8,128)S(1)} all-to-all(f32[8,48,128]{2,1,0:T(8,128)S(1)} %shard_map.113), channel_id=1, replica_groups=mesh['grp'=2,'tp'=16,'tok'=8] {'tok'}, dimensions={0} | all-to-all | bytes 393216 | tf_op jit(solution)/shard_map/all_to_all | solution.py:601
  140.7 4.9 %collective-permute-start.14 = (f32[80,128]{1,0:T(8,128)S(1)}, f32[80,128]{1,0:T(8,128)S(1)}, u32[]{:S(2)}, u32[]{:S(2)}) collective-permute-start(f32[80,128]{1,0:T(8,128)S(1)} %shard_map.114.mine), channel_id=1, source_target_pairs={{0,128},{1,129},{2,130},{3,131},{4,132},{5,133},{6,134},{7,135},{8... | collective-permute-start | bytes 122888 | tf_op jit(solution)/shard_map/ppermute | solution.py:36
  (65 shorter events, 19.1 us)
Async XLA Ops:
  0.6 4.1 %copy-start = (bf16[32,1024]{1,0:T(8,128)(2,1)S(1)}, bf16[32,1024]{1,0:T(8,128)(2,1)}, u32[]{:S(2)}) copy-start(bf16[32,1024]{1,0:T(8,128)(2,1)} %param.7) | copy-start | bytes 196612
  0.6 24.6 %collective-permute-start = (bf16[16,2,512,256]{3,2,1,0:T(8,128)(2,1)}, bf16[16,2,512,256]{3,2,1,0:T(8,128)(2,1)}, u32[]{:S(2)}, u32[]{:S(2)}) collective-permute-start(bf16[16,2,512,256]{3,2,1,0:T(8,128)(2,1)} %bitcast.22), channel_id=1, source_target_pairs={{0,128},{1,129},{2,130},{3,131},{4,132},{5,133},{6,134},{7,135},{8... | collective-permute-start | bytes 25165832 | tf_op jit(solution)/shard_map/ppermute | solution.py:36
  4.0 21.3 %collective-permute-start.1 = (bf16[16,2,128,256]{3,2,1,0:T(8,128)(2,1)}, bf16[16,2,128,256]{3,2,1,0:T(8,128)(2,1)S(1)}, u32[]{:S(2)}, u32[]{:S(2)}) collective-permute-start(bf16[16,2,128,256]{3,2,1,0:T(8,128)(2,1)} %bitcast.29), channel_id=1, source_target_pairs={{0,128},{1,129},{2,130},{3,131},{4,132},{5,133},{6,134},{7,135},{8... | collective-permute-start | bytes 6291464 | tf_op jit(solution)/shard_map/ppermute | solution.py:36
  5.5 19.7 %all-to-all-start = ((bf16[8,32,640]{2,1,0:T(8,128)(2,1)}), bf16[8,32,640]{2,1,0:T(8,128)(2,1)S(1)}, u32[]{:S(2)}, u32[]{:S(2)}) async-start(bf16[8,32,640]{2,1,0:T(8,128)(2,1)} %broadcast_in_dim.4), calls=%async_computation | async-start | bytes 655360 | tf_op jit(solution)/shard_map/all_to_all | solution.py:546
  19.4 29.8 %copy-start.11 = (f32[4096]{0:T(1024)S(1)}, f32[4096]{0:T(1024)}, u32[]{:S(2)}) copy-start(f32[4096]{0:T(1024)} %param.11) | copy-start | bytes 49156
  25.3 23.9 %copy-start.10 = (f32[32,512]{1,0:T(8,128)S(1)}, f32[32,512]{1,0:T(8,128)}, u32[]{:S(2)}) copy-start(f32[32,512]{1,0:T(8,128)} %reshape.45.refs_4_.refs_6_) | copy-start | bytes 196612
  25.5 3.8 %collective-permute-start.2 = (f32[8,256]{1,0:T(8,128)S(1)}, f32[8,256]{1,0:T(8,128)S(1)}, u32[]{:S(2)}, u32[]{:S(2)}) collective-permute-start(f32[8,256]{1,0:T(8,128)S(1)} %shard_map.103.mine), channel_id=1, source_target_pairs={{0,128},{1,129},{2,130},{3,131},{4,132},{5,133},{6,134},{7,135},{8... | collective-permute-start | bytes 24584 | tf_op jit(solution)/shard_map/ppermute | solution.py:36
  26.5 17.1 %collective-permute-start.4 = (bf16[256,640]{1,0:T(8,128)(2,1)S(1)}, bf16[256,640]{1,0:T(8,128)(2,1)S(1)}, u32[]{:S(2)}, u32[]{:S(2)}) collective-permute-start(bf16[256,640]{1,0:T(8,128)(2,1)S(1)} %bitcast.25), channel_id=1, source_target_pairs={{0,16},{1,17},{2,18},{3,19},{4,20},{5,21},{6,22},{7,23},{8,24},{9,... | collective-permute-start | bytes 983048 | tf_op jit(solution)/shard_map/ppermute | solution.py:36
  29.2 14.3 %collective-permute-start.5 = (bf16[256,640]{1,0:T(8,128)(2,1)S(1)}, bf16[256,640]{1,0:T(8,128)(2,1)S(1)}, u32[]{:S(2)}, u32[]{:S(2)}) collective-permute-start(bf16[256,640]{1,0:T(8,128)(2,1)S(1)} %bitcast.26), channel_id=1, source_target_pairs={{0,24},{1,25},{2,26},{3,27},{4,28},{5,29},{6,30},{7,31},{8,0},{9,1... | collective-permute-start | bytes 983048 | tf_op jit(solution)/shard_map/ppermute | solution.py:36
  30.1 13.6 %collective-permute-start.3 = (bf16[256,640]{1,0:T(8,128)(2,1)S(1)}, bf16[256,640]{1,0:T(8,128)(2,1)S(1)}, u32[]{:S(2)}, u32[]{:S(2)}) collective-permute-start(bf16[256,640]{1,0:T(8,128)(2,1)S(1)} %bitcast.27), channel_id=1, source_target_pairs={{0,8},{1,9},{2,10},{3,11},{4,12},{5,13},{6,14},{7,15},{8,16},{9,17... | collective-permute-start | bytes 983048 | tf_op jit(solution)/shard_map/ppermute | solution.py:36
  43.5 25.3 %copy-start.6 = (f32[256,1]{1,0:T(8,128)}, f32[256,1]{1,0:T(8,128)S(1)}, u32[]{:S(2)}) copy-start(f32[256,1]{1,0:T(8,128)S(1)} %get-tuple-element.61.refs_3_.refs_5_.r_s) | copy-start | bytes 3076
  43.7 11.0 %collective-permute-start.6 = (bf16[2,256,640]{2,1,0:T(8,128)(2,1)S(1)}, bf16[2,256,640]{2,1,0:T(8,128)(2,1)S(1)}, u32[]{:S(2)}, u32[]{:S(2)}) collective-permute-start(bf16[2,256,640]{2,1,0:T(8,128)(2,1)S(1)} %pad_maximum_fusion.refs_0_), channel_id=1, source_target_pairs={{0,32},{1,33},{2,34},{3,35},{4,36},{5,37},{6,38},{7,39},{8,40},{9,... | collective-permute-start | bytes 1966088 | tf_op jit(solution)/shard_map/ppermute | solution.py:36
  44.1 10.7 %collective-permute-start.7 = (bf16[2,256,640]{2,1,0:T(8,128)(2,1)S(1)}, bf16[2,256,640]{2,1,0:T(8,128)(2,1)S(1)}, u32[]{:S(2)}, u32[]{:S(2)}) collective-permute-start(bf16[2,256,640]{2,1,0:T(8,128)(2,1)S(1)} %pad_maximum_fusion.1.refs_1_), channel_id=1, source_target_pairs={{0,96},{1,97},{2,98},{3,99},{4,100},{5,101},{6,102},{7,103},{8,104... | collective-permute-start | bytes 1966088 | tf_op jit(solution)/shard_map/ppermute | solution.py:36
  46.5 15.3 %collective-permute-start.10 = (bf16[2,256,640]{2,1,0:T(8,128)(2,1)S(1)}, bf16[2,256,640]{2,1,0:T(8,128)(2,1)S(1)}, u32[]{:S(2)}, u32[]{:S(2)}) collective-permute-start(bf16[2,256,640]{2,1,0:T(8,128)(2,1)S(1)} %pad_maximum_fusion.1.refs_1_), channel_id=1, source_target_pairs={{0,32},{1,33},{2,34},{3,35},{4,36},{5,37},{6,38},{7,39},{8,40},{9,... | collective-permute-start | bytes 1966088 | tf_op jit(solution)/shard_map/ppermute | solution.py:36
  46.5 15.3 %collective-permute-start.11 = (bf16[2,256,640]{2,1,0:T(8,128)(2,1)S(1)}, bf16[2,256,640]{2,1,0:T(8,128)(2,1)S(1)}, u32[]{:S(2)}, u32[]{:S(2)}) collective-permute-start(bf16[2,256,640]{2,1,0:T(8,128)(2,1)S(1)} %pad_maximum_fusion.refs_0_), channel_id=1, source_target_pairs={{0,96},{1,97},{2,98},{3,99},{4,100},{5,101},{6,102},{7,103},{8,104... | collective-permute-start | bytes 1966088 | tf_op jit(solution)/shard_map/ppermute | solution.py:36
  54.8 14.0 %collective-permute-start.8 = (bf16[2,256,640]{2,1,0:T(8,128)(2,1)S(1)}, bf16[2,256,640]{2,1,0:T(8,128)(2,1)S(1)}, u32[]{:S(2)}, u32[]{:S(2)}) collective-permute-start(bf16[2,256,640]{2,1,0:T(8,128)(2,1)S(1)} %collective-permute-done.6.refs_0_), channel_id=1, source_target_pairs={{0,32},{1,33},{2,34},{3,35},{4,36},{5,37},{6,38},{7,39},{8,40},{9,... | collective-permute-start | bytes 1966088 | tf_op jit(solution)/shard_map/ppermute | solution.py:36
  54.8 14.0 %collective-permute-start.9 = (bf16[2,256,640]{2,1,0:T(8,128)(2,1)S(1)}, bf16[2,256,640]{2,1,0:T(8,128)(2,1)S(1)}, u32[]{:S(2)}, u32[]{:S(2)}) collective-permute-start(bf16[2,256,640]{2,1,0:T(8,128)(2,1)S(1)} %collective-permute-done.7.refs_3_), channel_id=1, source_target_pairs={{0,96},{1,97},{2,98},{3,99},{4,100},{5,101},{6,102},{7,103},{8,104... | collective-permute-start | bytes 1966088 | tf_op jit(solution)/shard_map/ppermute | solution.py:36
  68.8 11.0 %copy-start.12 = (s32[256]{0:T(256)S(1)}, s32[256]{0:T(256)}, u32[]{:S(2)}) copy-start(s32[256]{0:T(256)} %param.13) | copy-start | bytes 3076
  74.1 29.5 %copy-start.7 = (f32[256,1]{1,0:T(8,128)S(1)}, f32[256,1]{1,0:T(8,128)}, u32[]{:S(2)}) copy-start(f32[256,1]{1,0:T(8,128)} %copy-done.6) | copy-start | bytes 3076
  74.1 5.8 %collective-permute-start.12 = (f32[2,2,256,256]{3,2,1,0:T(8,128)}, f32[2,2,256,256]{3,2,1,0:T(8,128)}, u32[]{:S(2)}, u32[]{:S(2)}) collective-permute-start(f32[2,2,256,256]{3,2,1,0:T(8,128)} %get-tuple-element.79.mine), channel_id=1, source_target_pairs={{0,128},{1,129},{2,130},{3,131},{4,132},{5,133},{6,134},{7,135},{8... | collective-permute-start | bytes 3145736 | tf_op jit(solution)/shard_map/ppermute | solution.py:36
  77.2 4.8 %collective-permute-start.13 = (bf16[16,256,128]{2,1,0:T(8,128)(2,1)}, bf16[16,256,128]{2,1,0:T(8,128)(2,1)}, u32[]{:S(2)}, u32[]{:S(2)}) collective-permute-start(bf16[16,256,128]{2,1,0:T(8,128)(2,1)} %get-tuple-element.81.mine), channel_id=1, source_target_pairs={{0,128},{1,129},{2,130},{3,131},{4,132},{5,133},{6,134},{7,135},{8... | collective-permute-start | bytes 3145736 | tf_op jit(solution)/shard_map/ppermute | solution.py:36
  77.2 26.4 %copy-start.4 = (bf16[16,256,128]{2,1,0:T(8,128)(2,1)S(1)}, bf16[16,256,128]{2,1,0:T(8,128)(2,1)}, u32[]{:S(2)}) copy-start(bf16[16,256,128]{2,1,0:T(8,128)(2,1)} %copy-done.3) | copy-start | bytes 3145732
  107.9 20.2 %all-to-all-start.4 = ((bf16[16,288,128]{2,1,0:T(8,128)(2,1)}), bf16[16,288,128]{2,1,0:T(8,128)(2,1)}, u32[]{:S(2)}, u32[]{:S(2)}) async-start(bf16[16,288,128]{2,1,0:T(8,128)(2,1)} %copy-done.9), calls=%async_computation.4 | async-start | bytes 2359296 | tf_op jit(solution)/shard_map/all_to_all | solution.py:598
  140.7 5.8 %collective-permute-start.14 = (f32[80,128]{1,0:T(8,128)S(1)}, f32[80,128]{1,0:T(8,128)S(1)}, u32[]{:S(2)}, u32[]{:S(2)}) collective-permute-start(f32[80,128]{1,0:T(8,128)S(1)} %shard_map.114.mine), channel_id=1, source_target_pairs={{0,128},{1,129},{2,130},{3,131},{4,132},{5,133},{6,134},{7,135},{8... | collective-permute-start | bytes 122888 | tf_op jit(solution)/shard_map/ppermute | solution.py:36
  (6 other events, 11.2 us)
